TPU v7x, 128 devices: a whole 4x4x4 slice. The times are simulated.
128 devices in a mesh: plane: 8 (over z, core), dom: 16 (over x, y).
Axes of the slice: x: 4, y: 4, z: 4, core: 2. Of those that a mesh axis runs over, the one named last changes fastest.
Arguments:
- right_side: float32 [8, 32, 64, 640], P('plane', 'dom'), may hold values from -6 to 6
- inverse_diag: bfloat16 [8, 32, 640, 640], P('plane', 'dom'), may hold values from -0.25 to 0.25
- back_blocks: bfloat16 [8, 32, 2, 640, 640], P('plane', 'dom'), may hold values from -0.125 to 0.125
- back_near: int32 [8, 32, 2], P('plane', 'dom'), may hold values from 0 to 5
- fore_blocks: bfloat16 [8, 32, 2, 640, 640], P('plane', 'dom'), may hold values from -0.125 to 0.125
- fore_near: int32 [8, 32, 2], P('plane', 'dom'), may hold values from 0 to 5
- fringe_blocks: bfloat16 [8, 192, 640, 640], P('plane', 'dom'), may hold values from -0.25 to 0.25
- fringe_donor: int32 [8, 192], P('plane', 'dom'), may hold values from 0 to 1
- fringe_dest: int32 [8, 192, 1], P('plane', 'dom'), may hold values from 0 to 15; in each aligned block of 12 rows (0 to 11, 12 to 23, ..., all dimensions but the last counted through in order) at most 2 rows name the same one
- fringe_slot: int32 [8, 192], P('plane', 'dom'), may hold values from 0 to 1
Outputs:
- adjoint_update: bfloat16 [8, 32, 64, 640], P('plane', 'dom')
Inputs may be any that keep to these rules, and one draw needn't show every extreme that they name: `fringe_dest`: among the 12 links of one device, at most 2 name the same destination, and in some device exactly 2 do.
All inputs are finite; a program needn't handle non-finite values.
Results may differ from a plain program's by a relative error of at most 0.029.
Values may be sent and summed in bfloat16 or wider, within the bound.
A program may use at most 128 MiB of HBM per device.

v0:
```python
import jax
import jax.numpy as jnp
from jax import lax
from jax.sharding import PartitionSpec as P

CAPACITY = 2


def from_behind(block, axis, distance):
    devices = range(lax.axis_size(axis))
    route = [(i - distance, i) for i in devices if i - distance in devices]
    return lax.ppermute(block, axis, route)


def with_halo(cells, sides, width):
    for axis, dim in sides:
        count = lax.axis_size(axis)
        ends = count - 1
        head = lax.slice_in_dim(cells, 0, width, axis=dim)
        tail = lax.slice_in_dim(cells, cells.shape[dim] - width, cells.shape[dim], axis=dim)
        cells = jnp.concatenate(
            [
                lax.ppermute(tail, axis, [(i, (i + 1) % count) for i in range(ends)]),
                cells,
                lax.ppermute(head, axis, [((i + 1) % count, i) for i in range(ends)]),
            ],
            axis=dim,
        )
    return cells


def local_near(relative, dom_at, clusters, cluster_total):
    first_id = (dom_at - 1) * clusters
    global_ids = jnp.clip(first_id + relative, 0, cluster_total - 1)
    return global_ids - first_id


def couple(nearby, chosen, blocks):
    picked = nearby[chosen]
    return jnp.einsum("csoi,csij->coj", picked, blocks, preferred_element_type=jnp.float32)


def solve_block(vectors, inverse):
    return jnp.einsum("coi,cij->coj", vectors, inverse, preferred_element_type=jnp.float32)


def local(
    right_side,
    inverse_diag,
    back_blocks,
    back_near,
    fore_blocks,
    fore_near,
    fringe_blocks,
    fringe_donor,
    fringe_dest,
    fringe_slot,
):
    clusters = right_side.shape[1]
    objectives = right_side.shape[2]
    block_width = right_side.shape[3]
    link_count = fringe_blocks.shape[1]
    plane_count = lax.axis_size("plane")
    dom_count = lax.axis_size("dom")
    plane_at = lax.axis_index("plane")
    dom_at = lax.axis_index("dom")
    cluster_total = clusters * dom_count
    pieces = 1
    group_width = objectives // pieces
    inverse = inverse_diag[0]
    source = right_side[0].reshape(clusters, pieces, group_width, block_width)
    back_local = local_near(back_near[0], dom_at, clusters, cluster_total)
    fore_local = local_near(fore_near[0], dom_at, clusters, cluster_total)
    back_each = back_blocks[0]
    fore_each = fore_blocks[0]

    def upstream_turn(moment, carried):
        previous = jnp.clip(moment - 1 - plane_at, 0, pieces - 1)
        outgoing = lax.dynamic_index_in_dim(carried, previous, 1, keepdims=False)
        incoming = from_behind(outgoing, "plane", 1)
        nearby = with_halo(incoming, (("dom", 0),), clusters)
        block_at = moment - plane_at
        active = (block_at >= 0) & (block_at < pieces)
        block_safe = jnp.clip(block_at, 0, pieces - 1)

        def upstream_advance(operands):
            current, near_rows, index_at = operands
            rhs_part = lax.dynamic_index_in_dim(source, index_at, 1, keepdims=False)
            reduced = (rhs_part - couple(near_rows, back_local, back_each)).astype(jnp.bfloat16)
            solved = solve_block(reduced, inverse).astype(jnp.bfloat16)
            return lax.dynamic_update_index_in_dim(current, solved, index_at, 1)

        return lax.cond(
            active, upstream_advance, lambda operands: operands[0], (carried, nearby, block_safe)
        )

    zeros_state = jnp.zeros((clusters, pieces, group_width, block_width), jnp.bfloat16)
    forward = lax.fori_loop(0, plane_count + pieces - 1, upstream_turn, zeros_state)
    whole_forward = forward.reshape(clusters, objectives, block_width)
    donors = whole_forward[fringe_donor[0]]
    products = jnp.einsum(
        "loi,lij->loj", donors, fringe_blocks[0], preferred_element_type=jnp.float32
    ).astype(jnp.bfloat16)
    flat_products = products.reshape(link_count, objectives * block_width)
    destination = fringe_dest[0][:, 0]
    hits = (destination[:, None] == jnp.arange(dom_count)[None, :]).astype(jnp.int32)
    before = jnp.cumsum(hits, axis=0) - hits
    position = jnp.sum(before * hits, axis=1)
    place = destination * CAPACITY + position
    slot_ids = jnp.arange(dom_count * CAPACITY)
    select = (slot_ids[:, None] == place[None, :]).astype(jnp.bfloat16)
    packed = jnp.dot(select, flat_products, preferred_element_type=jnp.float32).astype(jnp.bfloat16)
    labels = jnp.dot(
        select, (fringe_slot[0] + 1).astype(jnp.bfloat16), preferred_element_type=jnp.float32
    ).astype(jnp.bfloat16)
    arrived, arrived_labels = (
        lax.all_to_all(
            packed.reshape(dom_count, CAPACITY, objectives * block_width),
            "dom",
            split_axis=0,
            concat_axis=0,
            tiled=True,
        ),
        lax.all_to_all(
            labels.reshape(dom_count, CAPACITY), "dom", split_axis=0, concat_axis=0, tiled=True
        ),
    )
    wanted = (jnp.arange(clusters) + 1).astype(jnp.bfloat16)
    receive = (arrived_labels.reshape(-1)[None, :] == wanted[:, None]).astype(jnp.bfloat16)
    fringe = jnp.dot(
        receive,
        arrived.reshape(dom_count * CAPACITY, objectives * block_width),
        preferred_element_type=jnp.float32,
    )
    fringe_split = fringe.reshape(clusters, pieces, group_width, block_width)

    def downstream_turn(moment, carried):
        offset_at = plane_count - 1 - plane_at
        previous = jnp.clip(moment - 1 - offset_at, 0, pieces - 1)
        outgoing = lax.dynamic_index_in_dim(carried, previous, 1, keepdims=False)
        incoming = from_behind(outgoing, "plane", -1)
        nearby = with_halo(incoming, (("dom", 0),), clusters)
        block_at = moment - offset_at
        active = (block_at >= 0) & (block_at < pieces)
        block_safe = jnp.clip(block_at, 0, pieces - 1)

        def downstream_advance(operands):
            current, near_rows, index_at = operands
            fringe_part = lax.dynamic_index_in_dim(fringe_split, index_at, 1, keepdims=False)
            upstream_part = lax.dynamic_index_in_dim(forward, index_at, 1, keepdims=False)
            summed = (fringe_part + couple(near_rows, fore_local, fore_each)).astype(jnp.bfloat16)
            updated = (upstream_part.astype(jnp.float32) - solve_block(summed, inverse)).astype(
                jnp.bfloat16
            )
            return lax.dynamic_update_index_in_dim(current, updated, index_at, 1)

        return lax.cond(
            active, downstream_advance, lambda operands: operands[0], (carried, nearby, block_safe)
        )

    backward = lax.fori_loop(0, plane_count + pieces - 1, downstream_turn, zeros_state)
    return backward.reshape(clusters, objectives, block_width)[None]


def solution(mesh):
    return jax.shard_map(
        local,
        mesh=mesh,
        in_specs=(
            P("plane", "dom", None, None),
            P("plane", "dom", None, None),
            P("plane", "dom", None, None, None),
            P("plane", "dom", None),
            P("plane", "dom", None, None, None),
            P("plane", "dom", None),
            P("plane", "dom", None, None),
            P("plane", "dom"),
            P("plane", "dom", None),
            P("plane", "dom"),
        ),
        out_specs=P("plane", "dom", None, None),
        check_vma=False,
    )
```

profile of v0, /device:TPU:2, one launch (start us, length us, event | category | flops | bytes accessed | tf_op | source)
XLA Modules:
  0.0 379.0 jit_solution(7258646367888517117)
XLA Ops:
  3.7 7.5 %all-to-all-start = ((bf16[16,1,2]{2,1,0:T(2,128)(2,1)}), bf16[16,1,2]{2,1,0:T(2,128)(2,1)S(1)}, u32[]{:S(2)}, u32[]{:S(2)}) async-start(bf16[16,1,2]{2,1,0:T(2,128)(2,1)} %all_to_all.12), calls=%async_computation | async-start | bytes 16384 | tf_op jit(solution)/shard_map/all_to_all | solution.py:124
  12.6 147.4 %while.34 = (s32[]{:T(128)}, bf16[2,1,64,640]{3,2,0,1:T(8,128)(2,1)S(1)}, s32[]{:T(128)}, f32[2,1,64,640]{3,2,0,1:T(8,128)}, s32[2,2]{1,0:T(2,128)S(1)}, /*index...) while((s32[]{:T(128)}, bf16[2,1,64,640]{3,2,0,1:T(8,128)(2,1)S(1)}, ...), condition=%wide.region_5.6_spmd, body=%wide.region_2.5_spmd.sunk | while | flops 315311104 | bytes 9343371 | solution.py:98
  14.9 4.6 %collective-permute-start.1 = (bf16[2,64,640]{2,1,0:T(8,128)(2,1)S(1)}, bf16[2,64,640]{2,1,0:T(8,128)(2,1)S(1)}, u32[]{:S(2)}, u32[]{:S(2)}) collective-permute-start(bf16[2,64,640]{2,1,0:T(8,128)(2,1)S(1)} %collective-permute-done), channel_id=1, source_target_pairs={{1,0},{2,1},{3,2},{4,3},{5,4},{6,5},{7,6},{8,7},{9,8},{10,9},{11,1... | collective-permute-start | bytes 491528 | tf_op jit(solution)/shard_map/while/body/eval_jaxpr/ppermute | solution.py:25
  22.3 6.5 %collective-permute-done.2 = bf16[2,64,640]{2,1,0:T(8,128)(2,1)S(1)} collective-permute-done((bf16[2,64,640]{2,1,0:T(8,128)(2,1)S(1)}, bf16[2,64,640]{2,1,0:T(8,128)(2,1)S(1)}, u32[]{:S(2)}, u32[]{:S(2)}) %collective-permute-start.2) | collective-permute-done | bytes 163872 | tf_op jit(solution)/shard_map/while/body/eval_jaxpr/ppermute | solution.py:23
  28.9 4.2 %conditional.4 = (bf16[2,1,64,640]{3,2,0,1:T(8,128)(2,1)S(1)}) conditional(s32[]{:T(128)} %convert_element_type.97, bf16[2,1,64,640]{3,2,0,1:T(8,128)(2,1)S(1)} %get-tuple-element.565, (f32[2,1,64,640]{3,2,0,1:T(8,128)}, s32[2,2]{1,0:T(2,128)S(1)}, bf16[6,64,640]{2,1,0:T(8,128)(2,1)S(1)}, bf16[2,2,640,640]{3,2,1,0:T(8,128)(2,1)}, ...), branch_computations={%region_3.3_spmd, %region_4.4_spmd} | conditional | flops 314819584 | bytes 6393960 | solution.py:93
  37.3 3.9 %collective-permute-start.2 = (bf16[2,64,640]{2,1,0:T(8,128)(2,1)S(1)}, bf16[2,64,640]{2,1,0:T(8,128)(2,1)S(1)}, u32[]{:S(2)}, u32[]{:S(2)}) collective-permute-start(bf16[2,64,640]{2,1,0:T(8,128)(2,1)S(1)} %collective-permute-done), channel_id=1, source_target_pairs={{0,1},{1,2},{2,3},{3,4},{4,5},{5,6},{6,7},{7,8},{8,9},{9,10},{10,1... | collective-permute-start | bytes 491528 | tf_op jit(solution)/shard_map/while/body/eval_jaxpr/ppermute | solution.py:23
  42.6 4.0 %collective-permute-done.2 = bf16[2,64,640]{2,1,0:T(8,128)(2,1)S(1)} collective-permute-done((bf16[2,64,640]{2,1,0:T(8,128)(2,1)S(1)}, bf16[2,64,640]{2,1,0:T(8,128)(2,1)S(1)}, u32[]{:S(2)}, u32[]{:S(2)}) %collective-permute-start.2) | collective-permute-done | bytes 163872 | tf_op jit(solution)/shard_map/while/body/eval_jaxpr/ppermute | solution.py:23
  46.8 9.0 %collective-permute-start = (bf16[2,64,640]{2,1,0:T(8,128)(2,1)S(1)}, bf16[2,64,640]{2,1,0:T(8,128)(2,1)S(1)}, u32[]{:S(2)}, u32[]{:S(2)}) collective-permute-start(bf16[2,64,640]{2,1,0:T(8,128)(2,1)S(1)} %bitcast.100), channel_id=1, source_target_pairs={{0,16},{16,32},{32,48},{48,64},{64,80},{80,96},{96,112},{1,17},{17... | collective-permute-start | bytes 491528 | tf_op jit(solution)/shard_map/while/body/eval_jaxpr/ppermute | solution.py:12
  58.7 3.9 %collective-permute-start.2 = (bf16[2,64,640]{2,1,0:T(8,128)(2,1)S(1)}, bf16[2,64,640]{2,1,0:T(8,128)(2,1)S(1)}, u32[]{:S(2)}, u32[]{:S(2)}) collective-permute-start(bf16[2,64,640]{2,1,0:T(8,128)(2,1)S(1)} %collective-permute-done), channel_id=1, source_target_pairs={{0,1},{1,2},{2,3},{3,4},{4,5},{5,6},{6,7},{7,8},{8,9},{9,10},{10,1... | collective-permute-start | bytes 491528 | tf_op jit(solution)/shard_map/while/body/eval_jaxpr/ppermute | solution.py:23
  65.5 4.0 %collective-permute-done.2 = bf16[2,64,640]{2,1,0:T(8,128)(2,1)S(1)} collective-permute-done((bf16[2,64,640]{2,1,0:T(8,128)(2,1)S(1)}, bf16[2,64,640]{2,1,0:T(8,128)(2,1)S(1)}, u32[]{:S(2)}, u32[]{:S(2)}) %collective-permute-start.2) | collective-permute-done | bytes 163872 | tf_op jit(solution)/shard_map/while/body/eval_jaxpr/ppermute | solution.py:23
  74.6 3.9 %collective-permute-start.2 = (bf16[2,64,640]{2,1,0:T(8,128)(2,1)S(1)}, bf16[2,64,640]{2,1,0:T(8,128)(2,1)S(1)}, u32[]{:S(2)}, u32[]{:S(2)}) collective-permute-start(bf16[2,64,640]{2,1,0:T(8,128)(2,1)S(1)} %collective-permute-done), channel_id=1, source_target_pairs={{0,1},{1,2},{2,3},{3,4},{4,5},{5,6},{6,7},{7,8},{8,9},{9,10},{10,1... | collective-permute-start | bytes 491528 | tf_op jit(solution)/shard_map/while/body/eval_jaxpr/ppermute | solution.py:23
  79.9 4.0 %collective-permute-done.2 = bf16[2,64,640]{2,1,0:T(8,128)(2,1)S(1)} collective-permute-done((bf16[2,64,640]{2,1,0:T(8,128)(2,1)S(1)}, bf16[2,64,640]{2,1,0:T(8,128)(2,1)S(1)}, u32[]{:S(2)}, u32[]{:S(2)}) %collective-permute-start.2) | collective-permute-done | bytes 163872 | tf_op jit(solution)/shard_map/while/body/eval_jaxpr/ppermute | solution.py:23
  84.0 8.3 %collective-permute-start = (bf16[2,64,640]{2,1,0:T(8,128)(2,1)S(1)}, bf16[2,64,640]{2,1,0:T(8,128)(2,1)S(1)}, u32[]{:S(2)}, u32[]{:S(2)}) collective-permute-start(bf16[2,64,640]{2,1,0:T(8,128)(2,1)S(1)} %bitcast.100), channel_id=1, source_target_pairs={{0,16},{16,32},{32,48},{48,64},{64,80},{80,96},{96,112},{1,17},{17... | collective-permute-start | bytes 491528 | tf_op jit(solution)/shard_map/while/body/eval_jaxpr/ppermute | solution.py:12
  95.2 3.9 %collective-permute-start.2 = (bf16[2,64,640]{2,1,0:T(8,128)(2,1)S(1)}, bf16[2,64,640]{2,1,0:T(8,128)(2,1)S(1)}, u32[]{:S(2)}, u32[]{:S(2)}) collective-permute-start(bf16[2,64,640]{2,1,0:T(8,128)(2,1)S(1)} %collective-permute-done), channel_id=1, source_target_pairs={{0,1},{1,2},{2,3},{3,4},{4,5},{5,6},{6,7},{7,8},{8,9},{9,10},{10,1... | collective-permute-start | bytes 491528 | tf_op jit(solution)/shard_map/while/body/eval_jaxpr/ppermute | solution.py:23
  100.5 4.0 %collective-permute-done.2 = bf16[2,64,640]{2,1,0:T(8,128)(2,1)S(1)} collective-permute-done((bf16[2,64,640]{2,1,0:T(8,128)(2,1)S(1)}, bf16[2,64,640]{2,1,0:T(8,128)(2,1)S(1)}, u32[]{:S(2)}, u32[]{:S(2)}) %collective-permute-start.2) | collective-permute-done | bytes 163872 | tf_op jit(solution)/shard_map/while/body/eval_jaxpr/ppermute | solution.py:23
  104.7 5.6 %collective-permute-start = (bf16[2,64,640]{2,1,0:T(8,128)(2,1)S(1)}, bf16[2,64,640]{2,1,0:T(8,128)(2,1)S(1)}, u32[]{:S(2)}, u32[]{:S(2)}) collective-permute-start(bf16[2,64,640]{2,1,0:T(8,128)(2,1)S(1)} %bitcast.100), channel_id=1, source_target_pairs={{0,16},{16,32},{32,48},{48,64},{64,80},{80,96},{96,112},{1,17},{17... | collective-permute-start | bytes 491528 | tf_op jit(solution)/shard_map/while/body/eval_jaxpr/ppermute | solution.py:12
  113.2 3.9 %collective-permute-start.2 = (bf16[2,64,640]{2,1,0:T(8,128)(2,1)S(1)}, bf16[2,64,640]{2,1,0:T(8,128)(2,1)S(1)}, u32[]{:S(2)}, u32[]{:S(2)}) collective-permute-start(bf16[2,64,640]{2,1,0:T(8,128)(2,1)S(1)} %collective-permute-done), channel_id=1, source_target_pairs={{0,1},{1,2},{2,3},{3,4},{4,5},{5,6},{6,7},{7,8},{8,9},{9,10},{10,1... | collective-permute-start | bytes 491528 | tf_op jit(solution)/shard_map/while/body/eval_jaxpr/ppermute | solution.py:23
  118.5 4.0 %collective-permute-done.2 = bf16[2,64,640]{2,1,0:T(8,128)(2,1)S(1)} collective-permute-done((bf16[2,64,640]{2,1,0:T(8,128)(2,1)S(1)}, bf16[2,64,640]{2,1,0:T(8,128)(2,1)S(1)}, u32[]{:S(2)}, u32[]{:S(2)}) %collective-permute-start.2) | collective-permute-done | bytes 163872 | tf_op jit(solution)/shard_map/while/body/eval_jaxpr/ppermute | solution.py:23
  122.7 5.6 %collective-permute-start = (bf16[2,64,640]{2,1,0:T(8,128)(2,1)S(1)}, bf16[2,64,640]{2,1,0:T(8,128)(2,1)S(1)}, u32[]{:S(2)}, u32[]{:S(2)}) collective-permute-start(bf16[2,64,640]{2,1,0:T(8,128)(2,1)S(1)} %bitcast.100), channel_id=1, source_target_pairs={{0,16},{16,32},{32,48},{48,64},{64,80},{80,96},{96,112},{1,17},{17... | collective-permute-start | bytes 491528 | tf_op jit(solution)/shard_map/while/body/eval_jaxpr/ppermute | solution.py:12
  131.2 3.9 %collective-permute-start.2 = (bf16[2,64,640]{2,1,0:T(8,128)(2,1)S(1)}, bf16[2,64,640]{2,1,0:T(8,128)(2,1)S(1)}, u32[]{:S(2)}, u32[]{:S(2)}) collective-permute-start(bf16[2,64,640]{2,1,0:T(8,128)(2,1)S(1)} %collective-permute-done), channel_id=1, source_target_pairs={{0,1},{1,2},{2,3},{3,4},{4,5},{5,6},{6,7},{7,8},{8,9},{9,10},{10,1... | collective-permute-start | bytes 491528 | tf_op jit(solution)/shard_map/while/body/eval_jaxpr/ppermute | solution.py:23
  136.5 4.0 %collective-permute-done.2 = bf16[2,64,640]{2,1,0:T(8,128)(2,1)S(1)} collective-permute-done((bf16[2,64,640]{2,1,0:T(8,128)(2,1)S(1)}, bf16[2,64,640]{2,1,0:T(8,128)(2,1)S(1)}, u32[]{:S(2)}, u32[]{:S(2)}) %collective-permute-start.2) | collective-permute-done | bytes 163872 | tf_op jit(solution)/shard_map/while/body/eval_jaxpr/ppermute | solution.py:23
  140.6 7.1 %collective-permute-start = (bf16[2,64,640]{2,1,0:T(8,128)(2,1)S(1)}, bf16[2,64,640]{2,1,0:T(8,128)(2,1)S(1)}, u32[]{:S(2)}, u32[]{:S(2)}) collective-permute-start(bf16[2,64,640]{2,1,0:T(8,128)(2,1)S(1)} %bitcast.100), channel_id=1, source_target_pairs={{0,16},{16,32},{32,48},{48,64},{64,80},{80,96},{96,112},{1,17},{17... | collective-permute-start | bytes 491528 | tf_op jit(solution)/shard_map/while/body/eval_jaxpr/ppermute | solution.py:12
  150.6 3.9 %collective-permute-start.2 = (bf16[2,64,640]{2,1,0:T(8,128)(2,1)S(1)}, bf16[2,64,640]{2,1,0:T(8,128)(2,1)S(1)}, u32[]{:S(2)}, u32[]{:S(2)}) collective-permute-start(bf16[2,64,640]{2,1,0:T(8,128)(2,1)S(1)} %collective-permute-done), channel_id=1, source_target_pairs={{0,1},{1,2},{2,3},{3,4},{4,5},{5,6},{6,7},{7,8},{8,9},{9,10},{10,1... | collective-permute-start | bytes 491528 | tf_op jit(solution)/shard_map/while/body/eval_jaxpr/ppermute | solution.py:23
  155.9 4.0 %collective-permute-done.2 = bf16[2,64,640]{2,1,0:T(8,128)(2,1)S(1)} collective-permute-done((bf16[2,64,640]{2,1,0:T(8,128)(2,1)S(1)}, bf16[2,64,640]{2,1,0:T(8,128)(2,1)S(1)}, u32[]{:S(2)}, u32[]{:S(2)}) %collective-permute-start.2) | collective-permute-done | bytes 163872 | tf_op jit(solution)/shard_map/while/body/eval_jaxpr/ppermute | solution.py:23
  160.8 5.5 %fusion.14 = bf16[12,64,640]{2,1,0:T(8,128)(2,1)S(1)} fusion(bf16[12,64,640]{2,1,0:T(8,128)(2,1)S(1)} %gather_fusion.2, bf16[1,12,640,640]{3,2,1,0:T(8,128)(2,1)} %param.24), kind=kOutput, calls=%fused_computation.28 | convolution fusion | flops 629637120 | bytes 11796480 | tf_op jit(solution)/shard_map/loi,lij->loj/dot_general | solution.py:101
  171.0 4.8 %all-to-all-start.1 = ((bf16[16,2,40960]{2,1,0:T(2,128)(2,1)}), bf16[16,2,40960]{2,1,0:T(2,128)(2,1)S(1)}, u32[]{:S(2)}, u32[]{:S(2)}) async-start(bf16[16,2,40960]{2,1,0:T(2,128)(2,1)} %reshape.88), calls=%async_computation.1 | async-start | bytes 5242880 | tf_op jit(solution)/shard_map/all_to_all | solution.py:117
  176.0 29.9 %all-to-all-done.1 = bf16[16,2,40960]{2,1,0:T(2,128)(2,1)S(1)} async-done(((bf16[16,2,40960]{2,1,0:T(2,128)(2,1)}), bf16[16,2,40960]{2,1,0:T(2,128)(2,1)S(1)}, u32[]{:S(2)}, u32[]{:S(2)}) %all-to-all-start.1) | async-done | bytes 2621472 | tf_op jit(solution)/shard_map/all_to_all | solution.py:117
  210.8 167.5 %while.35 = (s32[]{:T(128)}, bf16[2,1,64,640]{3,2,0,1:T(8,128)(2,1)S(1)}, s32[]{:T(128)}, bf16[2,1,64,640]{3,2,0,1:T(8,128)(2,1)S(1)}, f32[2,1,64,640]{3,2,0,1:T...) while((s32[]{:T(128)}, ...), condition=%wide.region_9.10_spmd, body=%wide.region_6.9_spmd.sunk | while | flops 315474944 | bytes 9507227 | solution.py:161
  212.1 5.9 %collective-permute-done.3 = bf16[2,64,640]{2,1,0:T(8,128)(2,1)S(1)} collective-permute-done((bf16[2,64,640]{2,1,0:T(8,128)(2,1)S(1)}, bf16[2,64,640]{2,1,0:T(8,128)(2,1)S(1)}, u32[]{:S(2)}, u32[]{:S(2)}) %collective-permute-start.3) | collective-permute-done | bytes 163872 | tf_op jit(solution)/shard_map/while/body/eval_jaxpr/ppermute | solution.py:12
  218.0 4.5 %collective-permute-start.4 = (bf16[2,64,640]{2,1,0:T(8,128)(2,1)S(1)}, bf16[2,64,640]{2,1,0:T(8,128)(2,1)S(1)}, u32[]{:S(2)}, u32[]{:S(2)}) collective-permute-start(bf16[2,64,640]{2,1,0:T(8,128)(2,1)S(1)} %collective-permute-done.3), channel_id=1, source_target_pairs={{1,0},{2,1},{3,2},{4,3},{5,4},{6,5},{7,6},{8,7},{9,8},{10,9},{11,1... | collective-permute-start | bytes 491528 | tf_op jit(solution)/shard_map/while/body/eval_jaxpr/ppermute | solution.py:25
  225.3 6.5 %collective-permute-done.5 = bf16[2,64,640]{2,1,0:T(8,128)(2,1)S(1)} collective-permute-done((bf16[2,64,640]{2,1,0:T(8,128)(2,1)S(1)}, bf16[2,64,640]{2,1,0:T(8,128)(2,1)S(1)}, u32[]{:S(2)}, u32[]{:S(2)}) %collective-permute-start.5) | collective-permute-done | bytes 163872 | tf_op jit(solution)/shard_map/while/body/eval_jaxpr/ppermute | solution.py:23
  233.2 7.2 %collective-permute-done.3 = bf16[2,64,640]{2,1,0:T(8,128)(2,1)S(1)} collective-permute-done((bf16[2,64,640]{2,1,0:T(8,128)(2,1)S(1)}, bf16[2,64,640]{2,1,0:T(8,128)(2,1)S(1)}, u32[]{:S(2)}, u32[]{:S(2)}) %collective-permute-start.3) | collective-permute-done | bytes 163872 | tf_op jit(solution)/shard_map/while/body/eval_jaxpr/ppermute | solution.py:12
  242.3 3.9 %collective-permute-start.5 = (bf16[2,64,640]{2,1,0:T(8,128)(2,1)S(1)}, bf16[2,64,640]{2,1,0:T(8,128)(2,1)S(1)}, u32[]{:S(2)}, u32[]{:S(2)}) collective-permute-start(bf16[2,64,640]{2,1,0:T(8,128)(2,1)S(1)} %collective-permute-done.3), channel_id=1, source_target_pairs={{0,1},{1,2},{2,3},{3,4},{4,5},{5,6},{6,7},{7,8},{8,9},{9,10},{10,1... | collective-permute-start | bytes 491528 | tf_op jit(solution)/shard_map/while/body/eval_jaxpr/ppermute | solution.py:23
  247.6 4.0 %collective-permute-done.5 = bf16[2,64,640]{2,1,0:T(8,128)(2,1)S(1)} collective-permute-done((bf16[2,64,640]{2,1,0:T(8,128)(2,1)S(1)}, bf16[2,64,640]{2,1,0:T(8,128)(2,1)S(1)}, u32[]{:S(2)}, u32[]{:S(2)}) %collective-permute-start.5) | collective-permute-done | bytes 163872 | tf_op jit(solution)/shard_map/while/body/eval_jaxpr/ppermute | solution.py:23
  253.1 4.2 %collective-permute-done.3 = bf16[2,64,640]{2,1,0:T(8,128)(2,1)S(1)} collective-permute-done((bf16[2,64,640]{2,1,0:T(8,128)(2,1)S(1)}, bf16[2,64,640]{2,1,0:T(8,128)(2,1)S(1)}, u32[]{:S(2)}, u32[]{:S(2)}) %collective-permute-start.3) | collective-permute-done | bytes 163872 | tf_op jit(solution)/shard_map/while/body/eval_jaxpr/ppermute | solution.py:12
  259.2 3.9 %collective-permute-start.5 = (bf16[2,64,640]{2,1,0:T(8,128)(2,1)S(1)}, bf16[2,64,640]{2,1,0:T(8,128)(2,1)S(1)}, u32[]{:S(2)}, u32[]{:S(2)}) collective-permute-start(bf16[2,64,640]{2,1,0:T(8,128)(2,1)S(1)} %collective-permute-done.3), channel_id=1, source_target_pairs={{0,1},{1,2},{2,3},{3,4},{4,5},{5,6},{6,7},{7,8},{8,9},{9,10},{10,1... | collective-permute-start | bytes 491528 | tf_op jit(solution)/shard_map/while/body/eval_jaxpr/ppermute | solution.py:23
  264.4 4.0 %collective-permute-done.5 = bf16[2,64,640]{2,1,0:T(8,128)(2,1)S(1)} collective-permute-done((bf16[2,64,640]{2,1,0:T(8,128)(2,1)S(1)}, bf16[2,64,640]{2,1,0:T(8,128)(2,1)S(1)}, u32[]{:S(2)}, u32[]{:S(2)}) %collective-permute-start.5) | collective-permute-done | bytes 163872 | tf_op jit(solution)/shard_map/while/body/eval_jaxpr/ppermute | solution.py:23
  269.9 7.0 %collective-permute-done.3 = bf16[2,64,640]{2,1,0:T(8,128)(2,1)S(1)} collective-permute-done((bf16[2,64,640]{2,1,0:T(8,128)(2,1)S(1)}, bf16[2,64,640]{2,1,0:T(8,128)(2,1)S(1)}, u32[]{:S(2)}, u32[]{:S(2)}) %collective-permute-start.3) | collective-permute-done | bytes 163872 | tf_op jit(solution)/shard_map/while/body/eval_jaxpr/ppermute | solution.py:12
  284.1 4.0 %collective-permute-done.5 = bf16[2,64,640]{2,1,0:T(8,128)(2,1)S(1)} collective-permute-done((bf16[2,64,640]{2,1,0:T(8,128)(2,1)S(1)}, bf16[2,64,640]{2,1,0:T(8,128)(2,1)S(1)}, u32[]{:S(2)}, u32[]{:S(2)}) %collective-permute-start.5) | collective-permute-done | bytes 163872 | tf_op jit(solution)/shard_map/while/body/eval_jaxpr/ppermute | solution.py:23
  289.6 5.1 %collective-permute-done.3 = bf16[2,64,640]{2,1,0:T(8,128)(2,1)S(1)} collective-permute-done((bf16[2,64,640]{2,1,0:T(8,128)(2,1)S(1)}, bf16[2,64,640]{2,1,0:T(8,128)(2,1)S(1)}, u32[]{:S(2)}, u32[]{:S(2)}) %collective-permute-start.3) | collective-permute-done | bytes 163872 | tf_op jit(solution)/shard_map/while/body/eval_jaxpr/ppermute | solution.py:12
  301.9 4.0 %collective-permute-done.5 = bf16[2,64,640]{2,1,0:T(8,128)(2,1)S(1)} collective-permute-done((bf16[2,64,640]{2,1,0:T(8,128)(2,1)S(1)}, bf16[2,64,640]{2,1,0:T(8,128)(2,1)S(1)}, u32[]{:S(2)}, u32[]{:S(2)}) %collective-permute-start.5) | collective-permute-done | bytes 163872 | tf_op jit(solution)/shard_map/while/body/eval_jaxpr/ppermute | solution.py:23
  307.3 4.2 %collective-permute-done.3 = bf16[2,64,640]{2,1,0:T(8,128)(2,1)S(1)} collective-permute-done((bf16[2,64,640]{2,1,0:T(8,128)(2,1)S(1)}, bf16[2,64,640]{2,1,0:T(8,128)(2,1)S(1)}, u32[]{:S(2)}, u32[]{:S(2)}) %collective-permute-start.3) | collective-permute-done | bytes 163872 | tf_op jit(solution)/shard_map/while/body/eval_jaxpr/ppermute | solution.py:12
  313.5 3.9 %collective-permute-start.5 = (bf16[2,64,640]{2,1,0:T(8,128)(2,1)S(1)}, bf16[2,64,640]{2,1,0:T(8,128)(2,1)S(1)}, u32[]{:S(2)}, u32[]{:S(2)}) collective-permute-start(bf16[2,64,640]{2,1,0:T(8,128)(2,1)S(1)} %collective-permute-done.3), channel_id=1, source_target_pairs={{0,1},{1,2},{2,3},{3,4},{4,5},{5,6},{6,7},{7,8},{8,9},{9,10},{10,1... | collective-permute-start | bytes 491528 | tf_op jit(solution)/shard_map/while/body/eval_jaxpr/ppermute | solution.py:23
  318.8 4.0 %collective-permute-done.5 = bf16[2,64,640]{2,1,0:T(8,128)(2,1)S(1)} collective-permute-done((bf16[2,64,640]{2,1,0:T(8,128)(2,1)S(1)}, bf16[2,64,640]{2,1,0:T(8,128)(2,1)S(1)}, u32[]{:S(2)}, u32[]{:S(2)}) %collective-permute-start.5) | collective-permute-done | bytes 163872 | tf_op jit(solution)/shard_map/while/body/eval_jaxpr/ppermute | solution.py:23
  324.2 4.2 %collective-permute-done.3 = bf16[2,64,640]{2,1,0:T(8,128)(2,1)S(1)} collective-permute-done((bf16[2,64,640]{2,1,0:T(8,128)(2,1)S(1)}, bf16[2,64,640]{2,1,0:T(8,128)(2,1)S(1)}, u32[]{:S(2)}, u32[]{:S(2)}) %collective-permute-start.3) | collective-permute-done | bytes 163872 | tf_op jit(solution)/shard_map/while/body/eval_jaxpr/ppermute | solution.py:12
  335.6 4.0 %collective-permute-done.5 = bf16[2,64,640]{2,1,0:T(8,128)(2,1)S(1)} collective-permute-done((bf16[2,64,640]{2,1,0:T(8,128)(2,1)S(1)}, bf16[2,64,640]{2,1,0:T(8,128)(2,1)S(1)}, u32[]{:S(2)}, u32[]{:S(2)}) %collective-permute-start.5) | collective-permute-done | bytes 163872 | tf_op jit(solution)/shard_map/while/body/eval_jaxpr/ppermute | solution.py:23
  341.1 22.4 %collective-permute-done.3 = bf16[2,64,640]{2,1,0:T(8,128)(2,1)S(1)} collective-permute-done((bf16[2,64,640]{2,1,0:T(8,128)(2,1)S(1)}, bf16[2,64,640]{2,1,0:T(8,128)(2,1)S(1)}, u32[]{:S(2)}, u32[]{:S(2)}) %collective-permute-start.3) | collective-permute-done | bytes 163872 | tf_op jit(solution)/shard_map/while/body/eval_jaxpr/ppermute | solution.py:12
  370.6 4.0 %collective-permute-done.5 = bf16[2,64,640]{2,1,0:T(8,128)(2,1)S(1)} collective-permute-done((bf16[2,64,640]{2,1,0:T(8,128)(2,1)S(1)}, bf16[2,64,640]{2,1,0:T(8,128)(2,1)S(1)}, u32[]{:S(2)}, u32[]{:S(2)}) %collective-permute-start.5) | collective-permute-done | bytes 163872 | tf_op jit(solution)/shard_map/while/body/eval_jaxpr/ppermute | solution.py:23
  (123 shorter events, 120.0 us)
Async XLA Ops:
  3.7 167.2 %all-to-all-start = ((bf16[16,1,2]{2,1,0:T(2,128)(2,1)}), bf16[16,1,2]{2,1,0:T(2,128)(2,1)S(1)}, u32[]{:S(2)}, u32[]{:S(2)}) async-start(bf16[16,1,2]{2,1,0:T(2,128)(2,1)} %all_to_all.12), calls=%async_computation | async-start | bytes 16384 | tf_op jit(solution)/shard_map/all_to_all | solution.py:124
  14.9 7.4 %collective-permute-start.1 = (bf16[2,64,640]{2,1,0:T(8,128)(2,1)S(1)}, bf16[2,64,640]{2,1,0:T(8,128)(2,1)S(1)}, u32[]{:S(2)}, u32[]{:S(2)}) collective-permute-start(bf16[2,64,640]{2,1,0:T(8,128)(2,1)S(1)} %collective-permute-done), channel_id=1, source_target_pairs={{1,0},{2,1},{3,2},{4,3},{5,4},{6,5},{7,6},{8,7},{9,8},{10,9},{11,1... | collective-permute-start | bytes 491528 | tf_op jit(solution)/shard_map/while/body/eval_jaxpr/ppermute | solution.py:25
  19.5 9.3 %collective-permute-start.2 = (bf16[2,64,640]{2,1,0:T(8,128)(2,1)S(1)}, bf16[2,64,640]{2,1,0:T(8,128)(2,1)S(1)}, u32[]{:S(2)}, u32[]{:S(2)}) collective-permute-start(bf16[2,64,640]{2,1,0:T(8,128)(2,1)S(1)} %collective-permute-done), channel_id=1, source_target_pairs={{0,1},{1,2},{2,3},{3,4},{4,5},{5,6},{6,7},{7,8},{8,9},{9,10},{10,1... | collective-permute-start | bytes 491528 | tf_op jit(solution)/shard_map/while/body/eval_jaxpr/ppermute | solution.py:23
  35.4 7.2 %collective-permute-start.1 = (bf16[2,64,640]{2,1,0:T(8,128)(2,1)S(1)}, bf16[2,64,640]{2,1,0:T(8,128)(2,1)S(1)}, u32[]{:S(2)}, u32[]{:S(2)}) collective-permute-start(bf16[2,64,640]{2,1,0:T(8,128)(2,1)S(1)} %collective-permute-done), channel_id=1, source_target_pairs={{1,0},{2,1},{3,2},{4,3},{5,4},{6,5},{7,6},{8,7},{9,8},{10,9},{11,1... | collective-permute-start | bytes 491528 | tf_op jit(solution)/shard_map/while/body/eval_jaxpr/ppermute | solution.py:25
  37.3 9.3 %collective-permute-start.2 = (bf16[2,64,640]{2,1,0:T(8,128)(2,1)S(1)}, bf16[2,64,640]{2,1,0:T(8,128)(2,1)S(1)}, u32[]{:S(2)}, u32[]{:S(2)}) collective-permute-start(bf16[2,64,640]{2,1,0:T(8,128)(2,1)S(1)} %collective-permute-done), channel_id=1, source_target_pairs={{0,1},{1,2},{2,3},{3,4},{4,5},{5,6},{6,7},{7,8},{8,9},{9,10},{10,1... | collective-permute-start | bytes 491528 | tf_op jit(solution)/shard_map/while/body/eval_jaxpr/ppermute | solution.py:23
  46.8 10.0 %collective-permute-start = (bf16[2,64,640]{2,1,0:T(8,128)(2,1)S(1)}, bf16[2,64,640]{2,1,0:T(8,128)(2,1)S(1)}, u32[]{:S(2)}, u32[]{:S(2)}) collective-permute-start(bf16[2,64,640]{2,1,0:T(8,128)(2,1)S(1)} %bitcast.100), channel_id=1, source_target_pairs={{0,16},{16,32},{32,48},{48,64},{64,80},{80,96},{96,112},{1,17},{17... | collective-permute-start | bytes 491528 | tf_op jit(solution)/shard_map/while/body/eval_jaxpr/ppermute | solution.py:12
  56.8 8.7 %collective-permute-start.1 = (bf16[2,64,640]{2,1,0:T(8,128)(2,1)S(1)}, bf16[2,64,640]{2,1,0:T(8,128)(2,1)S(1)}, u32[]{:S(2)}, u32[]{:S(2)}) collective-permute-start(bf16[2,64,640]{2,1,0:T(8,128)(2,1)S(1)} %collective-permute-done), channel_id=1, source_target_pairs={{1,0},{2,1},{3,2},{4,3},{5,4},{6,5},{7,6},{8,7},{9,8},{10,9},{11,1... | collective-permute-start | bytes 491528 | tf_op jit(solution)/shard_map/while/body/eval_jaxpr/ppermute | solution.py:25
  58.7 10.8 %collective-permute-start.2 = (bf16[2,64,640]{2,1,0:T(8,128)(2,1)S(1)}, bf16[2,64,640]{2,1,0:T(8,128)(2,1)S(1)}, u32[]{:S(2)}, u32[]{:S(2)}) collective-permute-start(bf16[2,64,640]{2,1,0:T(8,128)(2,1)S(1)} %collective-permute-done), channel_id=1, source_target_pairs={{0,1},{1,2},{2,3},{3,4},{4,5},{5,6},{6,7},{7,8},{8,9},{9,10},{10,1... | collective-permute-start | bytes 491528 | tf_op jit(solution)/shard_map/while/body/eval_jaxpr/ppermute | solution.py:23
  69.6 3.0 collective-permute-start
  72.7 7.2 %collective-permute-start.1 = (bf16[2,64,640]{2,1,0:T(8,128)(2,1)S(1)}, bf16[2,64,640]{2,1,0:T(8,128)(2,1)S(1)}, u32[]{:S(2)}, u32[]{:S(2)}) collective-permute-start(bf16[2,64,640]{2,1,0:T(8,128)(2,1)S(1)} %collective-permute-done), channel_id=1, source_target_pairs={{1,0},{2,1},{3,2},{4,3},{5,4},{6,5},{7,6},{8,7},{9,8},{10,9},{11,1... | collective-permute-start | bytes 491528 | tf_op jit(solution)/shard_map/while/body/eval_jaxpr/ppermute | solution.py:25
  74.6 9.3 %collective-permute-start.2 = (bf16[2,64,640]{2,1,0:T(8,128)(2,1)S(1)}, bf16[2,64,640]{2,1,0:T(8,128)(2,1)S(1)}, u32[]{:S(2)}, u32[]{:S(2)}) collective-permute-start(bf16[2,64,640]{2,1,0:T(8,128)(2,1)S(1)} %collective-permute-done), channel_id=1, source_target_pairs={{0,1},{1,2},{2,3},{3,4},{4,5},{5,6},{6,7},{7,8},{8,9},{9,10},{10,1... | collective-permute-start | bytes 491528 | tf_op jit(solution)/shard_map/while/body/eval_jaxpr/ppermute | solution.py:23
  84.0 9.3 %collective-permute-start = (bf16[2,64,640]{2,1,0:T(8,128)(2,1)S(1)}, bf16[2,64,640]{2,1,0:T(8,128)(2,1)S(1)}, u32[]{:S(2)}, u32[]{:S(2)}) collective-permute-start(bf16[2,64,640]{2,1,0:T(8,128)(2,1)S(1)} %bitcast.100), channel_id=1, source_target_pairs={{0,16},{16,32},{32,48},{48,64},{64,80},{80,96},{96,112},{1,17},{17... | collective-permute-start | bytes 491528 | tf_op jit(solution)/shard_map/while/body/eval_jaxpr/ppermute | solution.py:12
  93.3 7.2 %collective-permute-start.1 = (bf16[2,64,640]{2,1,0:T(8,128)(2,1)S(1)}, bf16[2,64,640]{2,1,0:T(8,128)(2,1)S(1)}, u32[]{:S(2)}, u32[]{:S(2)}) collective-permute-start(bf16[2,64,640]{2,1,0:T(8,128)(2,1)S(1)} %collective-permute-done), channel_id=1, source_target_pairs={{1,0},{2,1},{3,2},{4,3},{5,4},{6,5},{7,6},{8,7},{9,8},{10,9},{11,1... | collective-permute-start | bytes 491528 | tf_op jit(solution)/shard_map/while/body/eval_jaxpr/ppermute | solution.py:25
  95.2 9.3 %collective-permute-start.2 = (bf16[2,64,640]{2,1,0:T(8,128)(2,1)S(1)}, bf16[2,64,640]{2,1,0:T(8,128)(2,1)S(1)}, u32[]{:S(2)}, u32[]{:S(2)}) collective-permute-start(bf16[2,64,640]{2,1,0:T(8,128)(2,1)S(1)} %collective-permute-done), channel_id=1, source_target_pairs={{0,1},{1,2},{2,3},{3,4},{4,5},{5,6},{6,7},{7,8},{8,9},{9,10},{10,1... | collective-permute-start | bytes 491528 | tf_op jit(solution)/shard_map/while/body/eval_jaxpr/ppermute | solution.py:23
  104.7 6.6 %collective-permute-start = (bf16[2,64,640]{2,1,0:T(8,128)(2,1)S(1)}, bf16[2,64,640]{2,1,0:T(8,128)(2,1)S(1)}, u32[]{:S(2)}, u32[]{:S(2)}) collective-permute-start(bf16[2,64,640]{2,1,0:T(8,128)(2,1)S(1)} %bitcast.100), channel_id=1, source_target_pairs={{0,16},{16,32},{32,48},{48,64},{64,80},{80,96},{96,112},{1,17},{17... | collective-permute-start | bytes 491528 | tf_op jit(solution)/shard_map/while/body/eval_jaxpr/ppermute | solution.py:12
  111.3 7.2 %collective-permute-start.1 = (bf16[2,64,640]{2,1,0:T(8,128)(2,1)S(1)}, bf16[2,64,640]{2,1,0:T(8,128)(2,1)S(1)}, u32[]{:S(2)}, u32[]{:S(2)}) collective-permute-start(bf16[2,64,640]{2,1,0:T(8,128)(2,1)S(1)} %collective-permute-done), channel_id=1, source_target_pairs={{1,0},{2,1},{3,2},{4,3},{5,4},{6,5},{7,6},{8,7},{9,8},{10,9},{11,1... | collective-permute-start | bytes 491528 | tf_op jit(solution)/shard_map/while/body/eval_jaxpr/ppermute | solution.py:25
  113.2 9.3 %collective-permute-start.2 = (bf16[2,64,640]{2,1,0:T(8,128)(2,1)S(1)}, bf16[2,64,640]{2,1,0:T(8,128)(2,1)S(1)}, u32[]{:S(2)}, u32[]{:S(2)}) collective-permute-start(bf16[2,64,640]{2,1,0:T(8,128)(2,1)S(1)} %collective-permute-done), channel_id=1, source_target_pairs={{0,1},{1,2},{2,3},{3,4},{4,5},{5,6},{6,7},{7,8},{8,9},{9,10},{10,1... | collective-permute-start | bytes 491528 | tf_op jit(solution)/shard_map/while/body/eval_jaxpr/ppermute | solution.py:23
  122.7 6.6 %collective-permute-start = (bf16[2,64,640]{2,1,0:T(8,128)(2,1)S(1)}, bf16[2,64,640]{2,1,0:T(8,128)(2,1)S(1)}, u32[]{:S(2)}, u32[]{:S(2)}) collective-permute-start(bf16[2,64,640]{2,1,0:T(8,128)(2,1)S(1)} %bitcast.100), channel_id=1, source_target_pairs={{0,16},{16,32},{32,48},{48,64},{64,80},{80,96},{96,112},{1,17},{17... | collective-permute-start | bytes 491528 | tf_op jit(solution)/shard_map/while/body/eval_jaxpr/ppermute | solution.py:12
  129.3 7.2 %collective-permute-start.1 = (bf16[2,64,640]{2,1,0:T(8,128)(2,1)S(1)}, bf16[2,64,640]{2,1,0:T(8,128)(2,1)S(1)}, u32[]{:S(2)}, u32[]{:S(2)}) collective-permute-start(bf16[2,64,640]{2,1,0:T(8,128)(2,1)S(1)} %collective-permute-done), channel_id=1, source_target_pairs={{1,0},{2,1},{3,2},{4,3},{5,4},{6,5},{7,6},{8,7},{9,8},{10,9},{11,1... | collective-permute-start | bytes 491528 | tf_op jit(solution)/shard_map/while/body/eval_jaxpr/ppermute | solution.py:25
  131.2 9.3 %collective-permute-start.2 = (bf16[2,64,640]{2,1,0:T(8,128)(2,1)S(1)}, bf16[2,64,640]{2,1,0:T(8,128)(2,1)S(1)}, u32[]{:S(2)}, u32[]{:S(2)}) collective-permute-start(bf16[2,64,640]{2,1,0:T(8,128)(2,1)S(1)} %collective-permute-done), channel_id=1, source_target_pairs={{0,1},{1,2},{2,3},{3,4},{4,5},{5,6},{6,7},{7,8},{8,9},{9,10},{10,1... | collective-permute-start | bytes 491528 | tf_op jit(solution)/shard_map/while/body/eval_jaxpr/ppermute | solution.py:23
  140.6 8.1 %collective-permute-start = (bf16[2,64,640]{2,1,0:T(8,128)(2,1)S(1)}, bf16[2,64,640]{2,1,0:T(8,128)(2,1)S(1)}, u32[]{:S(2)}, u32[]{:S(2)}) collective-permute-start(bf16[2,64,640]{2,1,0:T(8,128)(2,1)S(1)} %bitcast.100), channel_id=1, source_target_pairs={{0,16},{16,32},{32,48},{48,64},{64,80},{80,96},{96,112},{1,17},{17... | collective-permute-start | bytes 491528 | tf_op jit(solution)/shard_map/while/body/eval_jaxpr/ppermute | solution.py:12
  148.7 7.2 %collective-permute-start.1 = (bf16[2,64,640]{2,1,0:T(8,128)(2,1)S(1)}, bf16[2,64,640]{2,1,0:T(8,128)(2,1)S(1)}, u32[]{:S(2)}, u32[]{:S(2)}) collective-permute-start(bf16[2,64,640]{2,1,0:T(8,128)(2,1)S(1)} %collective-permute-done), channel_id=1, source_target_pairs={{1,0},{2,1},{3,2},{4,3},{5,4},{6,5},{7,6},{8,7},{9,8},{10,9},{11,1... | collective-permute-start | bytes 491528 | tf_op jit(solution)/shard_map/while/body/eval_jaxpr/ppermute | solution.py:25
  150.6 9.3 %collective-permute-start.2 = (bf16[2,64,640]{2,1,0:T(8,128)(2,1)S(1)}, bf16[2,64,640]{2,1,0:T(8,128)(2,1)S(1)}, u32[]{:S(2)}, u32[]{:S(2)}) collective-permute-start(bf16[2,64,640]{2,1,0:T(8,128)(2,1)S(1)} %collective-permute-done), channel_id=1, source_target_pairs={{0,1},{1,2},{2,3},{3,4},{4,5},{5,6},{6,7},{7,8},{8,9},{9,10},{10,1... | collective-permute-start | bytes 491528 | tf_op jit(solution)/shard_map/while/body/eval_jaxpr/ppermute | solution.py:23
  171.0 34.9 %all-to-all-start.1 = ((bf16[16,2,40960]{2,1,0:T(2,128)(2,1)}), bf16[16,2,40960]{2,1,0:T(2,128)(2,1)S(1)}, u32[]{:S(2)}, u32[]{:S(2)}) async-start(bf16[16,2,40960]{2,1,0:T(2,128)(2,1)} %reshape.88), calls=%async_computation.1 | async-start | bytes 5242880 | tf_op jit(solution)/shard_map/all_to_all | solution.py:117
  210.8 7.2 %collective-permute-start.3 = (bf16[2,64,640]{2,1,0:T(8,128)(2,1)S(1)}, bf16[2,64,640]{2,1,0:T(8,128)(2,1)S(1)}, u32[]{:S(2)}, u32[]{:S(2)}) collective-permute-start(bf16[2,64,640]{2,1,0:T(8,128)(2,1)S(1)} %bitcast.106), channel_id=1, source_target_pairs={{16,0},{32,16},{48,32},{64,48},{80,64},{96,80},{112,96},{17,1},{33... | collective-permute-start | bytes 491528 | tf_op jit(solution)/shard_map/while/body/eval_jaxpr/ppermute | solution.py:12
  218.0 7.3 %collective-permute-start.4 = (bf16[2,64,640]{2,1,0:T(8,128)(2,1)S(1)}, bf16[2,64,640]{2,1,0:T(8,128)(2,1)S(1)}, u32[]{:S(2)}, u32[]{:S(2)}) collective-permute-start(bf16[2,64,640]{2,1,0:T(8,128)(2,1)S(1)} %collective-permute-done.3), channel_id=1, source_target_pairs={{1,0},{2,1},{3,2},{4,3},{5,4},{6,5},{7,6},{8,7},{9,8},{10,9},{11,1... | collective-permute-start | bytes 491528 | tf_op jit(solution)/shard_map/while/body/eval_jaxpr/ppermute | solution.py:25
  222.5 9.3 %collective-permute-start.5 = (bf16[2,64,640]{2,1,0:T(8,128)(2,1)S(1)}, bf16[2,64,640]{2,1,0:T(8,128)(2,1)S(1)}, u32[]{:S(2)}, u32[]{:S(2)}) collective-permute-start(bf16[2,64,640]{2,1,0:T(8,128)(2,1)S(1)} %collective-permute-done.3), channel_id=1, source_target_pairs={{0,1},{1,2},{2,3},{3,4},{4,5},{5,6},{6,7},{7,8},{8,9},{9,10},{10,1... | collective-permute-start | bytes 491528 | tf_op jit(solution)/shard_map/while/body/eval_jaxpr/ppermute | solution.py:23
  231.9 8.5 %collective-permute-start.3 = (bf16[2,64,640]{2,1,0:T(8,128)(2,1)S(1)}, bf16[2,64,640]{2,1,0:T(8,128)(2,1)S(1)}, u32[]{:S(2)}, u32[]{:S(2)}) collective-permute-start(bf16[2,64,640]{2,1,0:T(8,128)(2,1)S(1)} %bitcast.106), channel_id=1, source_target_pairs={{16,0},{32,16},{48,32},{64,48},{80,64},{96,80},{112,96},{17,1},{33... | collective-permute-start | bytes 491528 | tf_op jit(solution)/shard_map/while/body/eval_jaxpr/ppermute | solution.py:12
  240.4 7.2 %collective-permute-start.4 = (bf16[2,64,640]{2,1,0:T(8,128)(2,1)S(1)}, bf16[2,64,640]{2,1,0:T(8,128)(2,1)S(1)}, u32[]{:S(2)}, u32[]{:S(2)}) collective-permute-start(bf16[2,64,640]{2,1,0:T(8,128)(2,1)S(1)} %collective-permute-done.3), channel_id=1, source_target_pairs={{1,0},{2,1},{3,2},{4,3},{5,4},{6,5},{7,6},{8,7},{9,8},{10,9},{11,1... | collective-permute-start | bytes 491528 | tf_op jit(solution)/shard_map/while/body/eval_jaxpr/ppermute | solution.py:25
  242.3 9.3 %collective-permute-start.5 = (bf16[2,64,640]{2,1,0:T(8,128)(2,1)S(1)}, bf16[2,64,640]{2,1,0:T(8,128)(2,1)S(1)}, u32[]{:S(2)}, u32[]{:S(2)}) collective-permute-start(bf16[2,64,640]{2,1,0:T(8,128)(2,1)S(1)} %collective-permute-done.3), channel_id=1, source_target_pairs={{0,1},{1,2},{2,3},{3,4},{4,5},{5,6},{6,7},{7,8},{8,9},{9,10},{10,1... | collective-permute-start | bytes 491528 | tf_op jit(solution)/shard_map/while/body/eval_jaxpr/ppermute | solution.py:23
  251.8 5.5 %collective-permute-start.3 = (bf16[2,64,640]{2,1,0:T(8,128)(2,1)S(1)}, bf16[2,64,640]{2,1,0:T(8,128)(2,1)S(1)}, u32[]{:S(2)}, u32[]{:S(2)}) collective-permute-start(bf16[2,64,640]{2,1,0:T(8,128)(2,1)S(1)} %bitcast.106), channel_id=1, source_target_pairs={{16,0},{32,16},{48,32},{64,48},{80,64},{96,80},{112,96},{17,1},{33... | collective-permute-start | bytes 491528 | tf_op jit(solution)/shard_map/while/body/eval_jaxpr/ppermute | solution.py:12
  257.2 7.2 %collective-permute-start.4 = (bf16[2,64,640]{2,1,0:T(8,128)(2,1)S(1)}, bf16[2,64,640]{2,1,0:T(8,128)(2,1)S(1)}, u32[]{:S(2)}, u32[]{:S(2)}) collective-permute-start(bf16[2,64,640]{2,1,0:T(8,128)(2,1)S(1)} %collective-permute-done.3), channel_id=1, source_target_pairs={{1,0},{2,1},{3,2},{4,3},{5,4},{6,5},{7,6},{8,7},{9,8},{10,9},{11,1... | collective-permute-start | bytes 491528 | tf_op jit(solution)/shard_map/while/body/eval_jaxpr/ppermute | solution.py:25
  259.2 9.3 %collective-permute-start.5 = (bf16[2,64,640]{2,1,0:T(8,128)(2,1)S(1)}, bf16[2,64,640]{2,1,0:T(8,128)(2,1)S(1)}, u32[]{:S(2)}, u32[]{:S(2)}) collective-permute-start(bf16[2,64,640]{2,1,0:T(8,128)(2,1)S(1)} %collective-permute-done.3), channel_id=1, source_target_pairs={{0,1},{1,2},{2,3},{3,4},{4,5},{5,6},{6,7},{7,8},{8,9},{9,10},{10,1... | collective-permute-start | bytes 491528 | tf_op jit(solution)/shard_map/while/body/eval_jaxpr/ppermute | solution.py:23
  268.6 8.3 %collective-permute-start.3 = (bf16[2,64,640]{2,1,0:T(8,128)(2,1)S(1)}, bf16[2,64,640]{2,1,0:T(8,128)(2,1)S(1)}, u32[]{:S(2)}, u32[]{:S(2)}) collective-permute-start(bf16[2,64,640]{2,1,0:T(8,128)(2,1)S(1)} %bitcast.106), channel_id=1, source_target_pairs={{16,0},{32,16},{48,32},{64,48},{80,64},{96,80},{112,96},{17,1},{33... | collective-permute-start | bytes 491528 | tf_op jit(solution)/shard_map/while/body/eval_jaxpr/ppermute | solution.py:12
  276.9 7.2 %collective-permute-start.4 = (bf16[2,64,640]{2,1,0:T(8,128)(2,1)S(1)}, bf16[2,64,640]{2,1,0:T(8,128)(2,1)S(1)}, u32[]{:S(2)}, u32[]{:S(2)}) collective-permute-start(bf16[2,64,640]{2,1,0:T(8,128)(2,1)S(1)} %collective-permute-done.3), channel_id=1, source_target_pairs={{1,0},{2,1},{3,2},{4,3},{5,4},{6,5},{7,6},{8,7},{9,8},{10,9},{11,1... | collective-permute-start | bytes 491528 | tf_op jit(solution)/shard_map/while/body/eval_jaxpr/ppermute | solution.py:25
  278.9 9.3 %collective-permute-start.5 = (bf16[2,64,640]{2,1,0:T(8,128)(2,1)S(1)}, bf16[2,64,640]{2,1,0:T(8,128)(2,1)S(1)}, u32[]{:S(2)}, u32[]{:S(2)}) collective-permute-start(bf16[2,64,640]{2,1,0:T(8,128)(2,1)S(1)} %collective-permute-done.3), channel_id=1, source_target_pairs={{0,1},{1,2},{2,3},{3,4},{4,5},{5,6},{6,7},{7,8},{8,9},{9,10},{10,1... | collective-permute-start | bytes 491528 | tf_op jit(solution)/shard_map/while/body/eval_jaxpr/ppermute | solution.py:23
  288.3 6.4 %collective-permute-start.3 = (bf16[2,64,640]{2,1,0:T(8,128)(2,1)S(1)}, bf16[2,64,640]{2,1,0:T(8,128)(2,1)S(1)}, u32[]{:S(2)}, u32[]{:S(2)}) collective-permute-start(bf16[2,64,640]{2,1,0:T(8,128)(2,1)S(1)} %bitcast.106), channel_id=1, source_target_pairs={{16,0},{32,16},{48,32},{64,48},{80,64},{96,80},{112,96},{17,1},{33... | collective-permute-start | bytes 491528 | tf_op jit(solution)/shard_map/while/body/eval_jaxpr/ppermute | solution.py:12
  294.7 7.2 %collective-permute-start.4 = (bf16[2,64,640]{2,1,0:T(8,128)(2,1)S(1)}, bf16[2,64,640]{2,1,0:T(8,128)(2,1)S(1)}, u32[]{:S(2)}, u32[]{:S(2)}) collective-permute-start(bf16[2,64,640]{2,1,0:T(8,128)(2,1)S(1)} %collective-permute-done.3), channel_id=1, source_target_pairs={{1,0},{2,1},{3,2},{4,3},{5,4},{6,5},{7,6},{8,7},{9,8},{10,9},{11,1... | collective-permute-start | bytes 491528 | tf_op jit(solution)/shard_map/while/body/eval_jaxpr/ppermute | solution.py:25
  296.6 9.3 %collective-permute-start.5 = (bf16[2,64,640]{2,1,0:T(8,128)(2,1)S(1)}, bf16[2,64,640]{2,1,0:T(8,128)(2,1)S(1)}, u32[]{:S(2)}, u32[]{:S(2)}) collective-permute-start(bf16[2,64,640]{2,1,0:T(8,128)(2,1)S(1)} %collective-permute-done.3), channel_id=1, source_target_pairs={{0,1},{1,2},{2,3},{3,4},{4,5},{5,6},{6,7},{7,8},{8,9},{9,10},{10,1... | collective-permute-start | bytes 491528 | tf_op jit(solution)/shard_map/while/body/eval_jaxpr/ppermute | solution.py:23
  306.0 5.5 %collective-permute-start.3 = (bf16[2,64,640]{2,1,0:T(8,128)(2,1)S(1)}, bf16[2,64,640]{2,1,0:T(8,128)(2,1)S(1)}, u32[]{:S(2)}, u32[]{:S(2)}) collective-permute-start(bf16[2,64,640]{2,1,0:T(8,128)(2,1)S(1)} %bitcast.106), channel_id=1, source_target_pairs={{16,0},{32,16},{48,32},{64,48},{80,64},{96,80},{112,96},{17,1},{33... | collective-permute-start | bytes 491528 | tf_op jit(solution)/shard_map/while/body/eval_jaxpr/ppermute | solution.py:12
  311.6 7.2 %collective-permute-start.4 = (bf16[2,64,640]{2,1,0:T(8,128)(2,1)S(1)}, bf16[2,64,640]{2,1,0:T(8,128)(2,1)S(1)}, u32[]{:S(2)}, u32[]{:S(2)}) collective-permute-start(bf16[2,64,640]{2,1,0:T(8,128)(2,1)S(1)} %collective-permute-done.3), channel_id=1, source_target_pairs={{1,0},{2,1},{3,2},{4,3},{5,4},{6,5},{7,6},{8,7},{9,8},{10,9},{11,1... | collective-permute-start | bytes 491528 | tf_op jit(solution)/shard_map/while/body/eval_jaxpr/ppermute | solution.py:25
  313.5 9.3 %collective-permute-start.5 = (bf16[2,64,640]{2,1,0:T(8,128)(2,1)S(1)}, bf16[2,64,640]{2,1,0:T(8,128)(2,1)S(1)}, u32[]{:S(2)}, u32[]{:S(2)}) collective-permute-start(bf16[2,64,640]{2,1,0:T(8,128)(2,1)S(1)} %collective-permute-done.3), channel_id=1, source_target_pairs={{0,1},{1,2},{2,3},{3,4},{4,5},{5,6},{6,7},{7,8},{8,9},{9,10},{10,1... | collective-permute-start | bytes 491528 | tf_op jit(solution)/shard_map/while/body/eval_jaxpr/ppermute | solution.py:23
  322.9 5.5 %collective-permute-start.3 = (bf16[2,64,640]{2,1,0:T(8,128)(2,1)S(1)}, bf16[2,64,640]{2,1,0:T(8,128)(2,1)S(1)}, u32[]{:S(2)}, u32[]{:S(2)}) collective-permute-start(bf16[2,64,640]{2,1,0:T(8,128)(2,1)S(1)} %bitcast.106), channel_id=1, source_target_pairs={{16,0},{32,16},{48,32},{64,48},{80,64},{96,80},{112,96},{17,1},{33... | collective-permute-start | bytes 491528 | tf_op jit(solution)/shard_map/while/body/eval_jaxpr/ppermute | solution.py:12
  328.4 7.2 %collective-permute-start.4 = (bf16[2,64,640]{2,1,0:T(8,128)(2,1)S(1)}, bf16[2,64,640]{2,1,0:T(8,128)(2,1)S(1)}, u32[]{:S(2)}, u32[]{:S(2)}) collective-permute-start(bf16[2,64,640]{2,1,0:T(8,128)(2,1)S(1)} %collective-permute-done.3), channel_id=1, source_target_pairs={{1,0},{2,1},{3,2},{4,3},{5,4},{6,5},{7,6},{8,7},{9,8},{10,9},{11,1... | collective-permute-start | bytes 491528 | tf_op jit(solution)/shard_map/while/body/eval_jaxpr/ppermute | solution.py:25
  330.3 9.3 %collective-permute-start.5 = (bf16[2,64,640]{2,1,0:T(8,128)(2,1)S(1)}, bf16[2,64,640]{2,1,0:T(8,128)(2,1)S(1)}, u32[]{:S(2)}, u32[]{:S(2)}) collective-permute-start(bf16[2,64,640]{2,1,0:T(8,128)(2,1)S(1)} %collective-permute-done.3), channel_id=1, source_target_pairs={{0,1},{1,2},{2,3},{3,4},{4,5},{5,6},{6,7},{7,8},{8,9},{9,10},{10,1... | collective-permute-start | bytes 491528 | tf_op jit(solution)/shard_map/while/body/eval_jaxpr/ppermute | solution.py:23
  339.8 23.7 %collective-permute-start.3 = (bf16[2,64,640]{2,1,0:T(8,128)(2,1)S(1)}, bf16[2,64,640]{2,1,0:T(8,128)(2,1)S(1)}, u32[]{:S(2)}, u32[]{:S(2)}) collective-permute-start(bf16[2,64,640]{2,1,0:T(8,128)(2,1)S(1)} %bitcast.106), channel_id=1, source_target_pairs={{16,0},{32,16},{48,32},{64,48},{80,64},{96,80},{112,96},{17,1},{33... | collective-permute-start | bytes 491528 | tf_op jit(solution)/shard_map/while/body/eval_jaxpr/ppermute | solution.py:12
  363.4 7.2 %collective-permute-start.4 = (bf16[2,64,640]{2,1,0:T(8,128)(2,1)S(1)}, bf16[2,64,640]{2,1,0:T(8,128)(2,1)S(1)}, u32[]{:S(2)}, u32[]{:S(2)}) collective-permute-start(bf16[2,64,640]{2,1,0:T(8,128)(2,1)S(1)} %collective-permute-done.3), channel_id=1, source_target_pairs={{1,0},{2,1},{3,2},{4,3},{5,4},{6,5},{7,6},{8,7},{9,8},{10,9},{11,1... | collective-permute-start | bytes 491528 | tf_op jit(solution)/shard_map/while/body/eval_jaxpr/ppermute | solution.py:25
  365.3 9.3 %collective-permute-start.5 = (bf16[2,64,640]{2,1,0:T(8,128)(2,1)S(1)}, bf16[2,64,640]{2,1,0:T(8,128)(2,1)S(1)}, u32[]{:S(2)}, u32[]{:S(2)}) collective-permute-start(bf16[2,64,640]{2,1,0:T(8,128)(2,1)S(1)} %collective-permute-done.3), channel_id=1, source_target_pairs={{0,1},{1,2},{2,3},{3,4},{4,5},{5,6},{6,7},{7,8},{8,9},{9,10},{10,1... | collective-permute-start | bytes 491528 | tf_op jit(solution)/shard_map/while/body/eval_jaxpr/ppermute | solution.py:23
  (4 other events, 7.7 us)
where the time goes:
time: 381 us; the launch traced here: 379 us
  waiting for transfers between devices  190 us (50%)
  starting transfers between devices  157 us (41%)
  matrix products  15.7 us (4%)
  local copies, waits for them, and re-layouts  9.96 us (3%)
  other arithmetic  4.74 us (1%)
    ppermute x16, waiting for transfers between devices, with_halo(): lax.ppermute(tail, axis, [(i, (i + 1) % count) for i in range(ends)])  69.5 us
    ppermute x16, waiting for transfers between devices, from_behind(): return lax.ppermute(block, axis, route)  68.2 us
    ppermute x16, starting transfers between devices, with_halo(): lax.ppermute(tail, axis, [(i, (i + 1) % count) for i in range(ends)])  58.8 us
    ppermute x16, starting transfers between devices, from_behind(): return lax.ppermute(block, axis, route)  50.6 us
    ppermute x16, starting transfers between devices, with_halo(): lax.ppermute(head, axis, [((i + 1) % count, i) for i in range(ends)])  35.8 us
    all_to_all x1, waiting for transfers between devices, local(): lax.all_to_all(packed.reshape(dom_count, CAPACITY, objectives * block_wid...  29.9 us
    ppermute x16, waiting for transfers between devices, with_halo(): lax.ppermute(head, axis, [((i + 1) % count, i) for i in range(ends)])  22 us
  transfers between devices with their start and end apart: 50, of which 49 were waited for; matrix products, arithmetic and copies ran while one was open for 5% of the time, Pallas kernels for 0%

commit v1 on v0

v1 whole, which is shorter than its diff:
```python
import functools

import jax
import jax.numpy as jnp
from jax import lax
from jax.experimental import pallas as pl
from jax.experimental.pallas import tpu as pltpu
from jax.sharding import PartitionSpec as P

BF, F32 = jnp.bfloat16, jnp.float32
MESH = pl.DeviceIdType.MESH
PIECES = 4
ROWS = 16


def dot(a, b):
    return jnp.dot(a, b, preferred_element_type=F32)


def kernel(
    rhs_h, diag_h, back_h, fore_h, link_h, back_near, fore_near, donor, dest, slot,
    out,
    rhs, diag, back, fore, link, coup, base, w, xs, prod, pack, part, first, second,
    pick,
    near_u0, near_u1, near_u2, near_u3, near_d0, near_d1, near_d2, near_d3,
    load_sem, up_s, up_r, dn_s, dn_r, f1_s, f1_r, f2_s, f2_r,
):
    p, d = lax.axis_index("plane"), lax.axis_index("dom")
    x, y = d // 4, d % 4
    near_u = (near_u0, near_u1, near_u2, near_u3)
    near_d = (near_d0, near_d1, near_d2, near_d3)
    links = link.shape[0]

    loads = [
        pltpu.make_async_copy(h.at[0], v, load_sem.at[i])
        for i, (h, v) in enumerate(
            ((rhs_h, rhs), (diag_h, diag), (back_h, back), (link_h, link), (fore_h, fore))
        )
    ]
    load_rhs, load_diag, load_back, load_link, load_fore = loads
    load_rhs.start()
    load_diag.start()
    load_back.start()

    barrier = pltpu.get_barrier_semaphore()

    def greet(plane, dom):
        pl.semaphore_signal(
            barrier, inc=1, device_id={"plane": plane, "dom": dom}, device_id_type=MESH
        )

    for step in (-1, 1):
        @pl.when((p + step >= 0) & (p + step < 8))
        def _():
            greet(p + step, d)

            @pl.when(d > 0)
            def _():
                greet(p + step, d - 1)

            @pl.when(d < 15)
            def _():
                greet(p + step, d + 1)

    for j in (1, 2, 3):
        greet(p, x * 4 + (y + j) % 4)
        greet(p, ((x + j) % 4) * 4 + y)
    beside = jnp.where((d > 0) & (d < 15), 3, 2)
    planes = jnp.where((p > 0) & (p < 7), 2, 1)

    def moves(k, step, src, near, ss, rs):
        def one(n, shift):
            return pltpu.make_async_remote_copy(
                src_ref=src.at[k],
                dst_ref=near[k].at[pl.ds(2 - 2 * shift, 2)],
                send_sem=ss.at[k, n],
                recv_sem=rs.at[k, n],
                device_id={"plane": p + step, "dom": d + shift},
                device_id_type=MESH,
            )

        return one(0, 1), one(1, -1), one(2, 0)

    def move(act, k, step, src, near, ss, rs):
        right, left, same = moves(k, step, src, near, ss, rs)
        if act == "recv":
            pl.when(d > 0)(right.wait_recv)
            pl.when(d < 15)(left.wait_recv)
            same.wait_recv()
        else:
            do = (lambda c: c.start()) if act == "start" else (lambda c: c.wait_send())
            pl.when(d < 15)(lambda: do(right))
            pl.when(d > 0)(lambda: do(left))
            do(same)

    up = functools.partial(move, step=1, src=w, near=near_u, ss=up_s, rs=up_r)
    down = functools.partial(move, step=-1, src=xs, near=near_d, ss=dn_s, rs=dn_r)

    def spot(table, c, s):
        start = (d - 1) * 2
        return jnp.clip(start + table[0, c, s], 0, 31) - start

    load_rhs.wait()
    load_diag.wait()
    for c in range(2):
        whole = dot(rhs[c].astype(BF), diag[c])
        for k in range(PIECES):
            base[k, c] = whole[k * ROWS:(k + 1) * ROWS]

    pl.semaphore_wait(barrier, beside * planes + 6)

    @pl.when(p == 0)
    def _():
        for k in range(PIECES):
            w[k] = base[k].astype(BF)
            up("start", k)

    load_back.wait()
    load_link.start()
    load_fore.start()

    def compose(src, dst):
        def body(i, _):
            dst[i // 2, i % 2] = dot(src[i // 2, i % 2], diag[i // 2]).astype(BF)
            return 0

        lax.fori_loop(0, 4, body, 0)

    pl.when(p > 0)(lambda: compose(back, coup))

    def choose(i, _):
        one, two = jnp.int32(links), jnp.int32(links)
        for l in range(links):
            hit = dest[0, l] * 2 + slot[0, l] == i
            two = jnp.where(hit & (one < links), l, two)
            one = jnp.where(hit & (one == links), l, one)
        pick[0, i] = one
        pick[1, i] = two
        return 0

    lax.fori_loop(0, 32, choose, 0)
    for k in range(PIECES):
        prod[k, links] = jnp.zeros((ROWS, 640), BF)

    @pl.when(p >= 3)
    def _():
        load_fore.wait()
        pl.when(p < 7)(lambda: compose(fore, back))

    def up_step(k):
        up("recv", k)
        for c in range(2):
            total = base[k, c]
            for s in range(2):
                total = total - dot(near_u[k][spot(back_near, c, s)], coup[c, s])
            w[k, c] = total.astype(BF)

    def products(ks):
        def body(l, _):
            rows = jnp.concatenate([w[k, donor[0, l]] for k in ks], axis=0)
            got = dot(rows, link[l]).astype(BF)
            for i, k in enumerate(ks):
                prod[k, l] = got[i * ROWS:(i + 1) * ROWS]
            return 0

        lax.fori_loop(0, links, body, 0)

    def phase1(k):
        a = y if k % 2 == 0 else x
        found = []
        for j in (1, 2, 3):
            there = (a + j) % 4
            target = x * 4 + there if k % 2 == 0 else there * 4 + y
            found.append(pltpu.make_async_remote_copy(
                src_ref=pack.at[k, there],
                dst_ref=first.at[k, j - 1],
                send_sem=f1_s.at[k, j - 1],
                recv_sem=f1_r.at[k, j - 1],
                device_id={"plane": p, "dom": target},
                device_id_type=MESH,
            ))
        return a, found

    def phase2(k):
        b = x if k % 2 == 0 else y
        found = []
        for j in (1, 2, 3):
            there = (b + j) % 4
            target = there * 4 + y if k % 2 == 0 else x * 4 + there
            found.append(pltpu.make_async_remote_copy(
                src_ref=part.at[k, there],
                dst_ref=second.at[k, j - 1],
                send_sem=f2_s.at[k, j - 1],
                recv_sem=f2_r.at[k, j - 1],
                device_id={"plane": p, "dom": target},
                device_id_type=MESH,
            ))
        return b, found

    def send_first(k):
        def body(i, _):
            a, b, c = i // 8, (i // 2) % 4, i % 2
            cell = (b * 4 + a) * 2 + c if k % 2 == 0 else i
            both = prod[k, pick[0, cell]].astype(F32) + prod[k, pick[1, cell]].astype(F32)
            pack[k, a, b, c] = both.astype(BF)
            return 0

        lax.fori_loop(0, 32, body, 0)
        for copy in phase1(k)[1]:
            copy.start()

    def send_second(k):
        a, copies = phase1(k)
        for copy in copies:
            copy.wait_recv()

        def body(b, _):
            for c in range(2):
                total = pack[k, a, b, c].astype(F32)
                for j in range(3):
                    total = total + first[k, j, b, c].astype(F32)
                part[k, b, c] = total.astype(BF)
            return 0

        lax.fori_loop(0, 4, body, 0)
        for copy in phase2(k)[1]:
            copy.start()

    def settle(k):
        b, copies = phase2(k)
        for copy in copies:
            copy.wait_recv()
        for c in range(2):
            total = part[k, b, c].astype(F32)
            for j in range(3):
                total = total + second[k, j, c].astype(F32)
            base[k, c] = w[k, c].astype(F32) - dot(total.astype(BF), diag[c])

    def finish(k, c, value):
        value = value.astype(BF)
        xs[k, c] = value
        out[0, c, k * ROWS:(k + 1) * ROWS] = value

    def turn(k):
        for c in range(2):
            finish(k, c, base[k, c])
        down("start", k)

    def down_step(k):
        down("recv", k)
        for c in range(2):
            total = base[k, c]
            for s in range(2):
                total = total - dot(near_d[k][spot(fore_near, c, s)], back[c, s])
            finish(k, c, total)
        pl.when(p > 0)(lambda: down("start", k))

    @pl.when(p == 7)
    def _():
        load_link.wait()
        for k in range(PIECES):
            up_step(k)
            products((k,))
            send_first(k)
            if k >= 2:
                send_second(k - 2)
        for k in range(PIECES):
            settle(k)
            turn(k)
            if k < 2:
                send_second(k + 2)

    @pl.when(p < 7)
    def _():
        @pl.when(p > 0)
        def _():
            for k in range(PIECES):
                up_step(k)
                up("start", k)

        load_link.wait()
        products(tuple(range(PIECES)))
        for k in range(PIECES):
            send_first(k)
        for k in range(PIECES):
            send_second(k)

        @pl.when(p < 3)
        def _():
            load_fore.wait()
            compose(fore, back)

        for k in range(PIECES):
            settle(k)
            down_step(k)

    for k in range(PIECES):
        pl.when(p < 7)(lambda: up("sent", k))
        pl.when(p > 0)(lambda: down("sent", k))
        for copy in phase1(k)[1] + phase2(k)[1]:
            copy.wait_send()


def local(rhs, diag, back, back_near, fore, fore_near, link, donor, dest, slot):
    links = link.shape[1]
    piece = (PIECES, 2, ROWS, 640)
    near = pltpu.VMEM((6, ROWS, 640), BF)
    sems = pltpu.SemaphoreType.DMA((PIECES, 3))
    anywhere = pl.BlockSpec(memory_space=pl.ANY)
    scalars = pl.BlockSpec(memory_space=pltpu.SMEM)
    return pl.pallas_call(
        kernel,
        out_shape=jax.ShapeDtypeStruct(rhs.shape, BF),
        in_specs=[anywhere] * 5 + [scalars] * 5,
        out_specs=pl.BlockSpec(memory_space=pltpu.VMEM),
        scratch_shapes=[
            pltpu.VMEM(rhs.shape[1:], F32),
            pltpu.VMEM(diag.shape[1:], BF),
            pltpu.VMEM(back.shape[1:], BF),
            pltpu.VMEM(fore.shape[1:], BF),
            pltpu.VMEM(link.shape[1:], BF),
            pltpu.VMEM(back.shape[1:], BF),
            pltpu.VMEM(piece, F32),
            pltpu.VMEM(piece, BF),
            pltpu.VMEM(piece, BF),
            pltpu.VMEM((PIECES, links + 1, ROWS, 640), BF),
            pltpu.VMEM((PIECES, 4, 4, 2, ROWS, 640), BF),
            pltpu.VMEM((PIECES, 4, 2, ROWS, 640), BF),
            pltpu.VMEM((PIECES, 3, 4, 2, ROWS, 640), BF),
            pltpu.VMEM((PIECES, 3, 2, ROWS, 640), BF),
            pltpu.SMEM((2, 32), jnp.int32),
        ]
        + [near] * (2 * PIECES)
        + [pltpu.SemaphoreType.DMA((5,))]
        + [sems] * 8,
        compiler_params=pltpu.CompilerParams(
            collective_id=0, has_side_effects=True, vmem_limit_bytes=58 * 1024 * 1024
        ),
        cost_estimate=pl.CostEstimate(
            flops=2 * 32 * 640 * 640 * 640, bytes_accessed=20_000_000, transcendentals=0
        ),
    )(rhs, diag, back, fore, link, back_near, fore_near, donor, dest[:, :, 0], slot)


def solution(mesh):
    return jax.shard_map(
        local,
        mesh=mesh,
        in_specs=(
            P("plane", "dom", None, None),
            P("plane", "dom", None, None),
            P("plane", "dom", None, None, None),
            P("plane", "dom", None),
            P("plane", "dom", None, None, None),
            P("plane", "dom", None),
            P("plane", "dom", None, None),
            P("plane", "dom"),
            P("plane", "dom", None),
            P("plane", "dom"),
        ),
        out_specs=P("plane", "dom", None, None),
        check_vma=False,
    )
```

time: 381 us -> 103 us (0.27)
  waiting for transfers between devices: 190 us -> 0 us
  starting transfers between devices: 157 us -> 0 us
  Pallas kernels: 0 us -> 101 us
  matrix products: 15.7 us -> 0 us
  local copies, waits for them, and re-layouts: 9.96 us -> 1.6 us
  other arithmetic: 4.74 us -> 0 us
    ppermute x48 -> x0, waiting for transfers between devices: 160 us -> none  [the longest x16 69.5 us: with_halo(): lax.ppermute(tail, axis, [(i, (i + 1) % count) for i in range(ends)])]
    ppermute x48 -> x0, starting transfers between devices: 145 us -> none  [the longest x16 58.8 us: with_halo(): lax.ppermute(tail, axis, [(i, (i + 1) % count) for i in range(ends)])]
    pallas_call x0 -> x1, Pallas kernels: none -> 101 us  [local(): pl.pallas_call(kernel, out_shape=jax.ShapeDtypeStruct(rhs.shape, BF), in_...]
    all_to_all x2 -> x0, waiting for transfers between devices: 29.9 us -> none  [the longest x1 29.9 us: local(): lax.all_to_all(packed.reshape(dom_count, CAPACITY, objectives * block_wid...]
    dot_general x6 -> x0, matrix products: 15.7 us -> none  [the longest x2 6.27 us: solve_block(): jnp.einsum('coi,cij->coj', vectors, inverse, preferred_element_type=jnp.f...]
    all_to_all x2 -> x0, starting transfers between devices: 12.3 us -> none  [the longest x1 7.48 us: local(): lax.all_to_all(labels.reshape(dom_count, CAPACITY), 'dom', split_axis=0,...]
    reshape x2 -> x0, local copies, waits for them, and re-layouts: 5.47 us -> none  [the longest x1 2.99 us: local(): packed.reshape(dom_count, CAPACITY, objectives * block_width)]
  transfers between devices with their start and end apart: 50 -> 0, of which waited for: 49 -> 0; matrix products, arithmetic and copies ran while one was open for 5% -> 0% of each run, Pallas kernels for 0% -> 0%
where the time goes in v1:
time: 103 us
  Pallas kernels  101 us (98%)
  local copies, waits for them, and re-layouts  1.6 us (2%)
    pallas_call x1, Pallas kernels, local(): pl.pallas_call(kernel, out_shape=jax.ShapeDtypeStruct(rhs.shape, BF), in_...  101 us

profile of v1, /device:TPU:2, one launch (start us, length us, event | category | flops | bytes accessed | tf_op | source)
XLA Modules:
  0.0 102.5 jit_solution(8985073642192511079)
XLA Ops:
  0.0 100.9 %shard_map.100 = bf16[1,2,64,640]{3,2,1,0:T(8,128)(2,1)} custom-call(f32[1,2,64,640]{3,2,1,0:T(8,128)} %rhs_h.1, bf16[1,2,640,640]{3,2,1,0:T(8,128)(2,1)} %diag_h.1, bf16[1,2,2,640,640]{4,3,2,1,0:T(8,128)(2,1)} %back_h.1, bf16[1,2,2,640,640]{4,3,2,1,0:T(8,128)(2,1)} %fore_h.1, bf16[1,12,640,640]{3,2,1,0:T(8,128)(2,1)} %link_h.1, s32[1,2,2]{2,1,0:T(2,128)} %back_near.1, ...), custom_call_target="tpu_custom_call" | custom-call | flops 16777216000 | bytes 20000000 | tf_op jit(solution)/shard_map/pallas_call | solution.py:311
  100.9 1.6 %copy.12 = bf16[1,2,64,640]{3,2,1,0:T(8,128)(2,1)} copy(bf16[1,2,64,640]{3,2,1,0:T(8,128)(2,1)} %shard_map.100) | data formatting | bytes 327680

commit v2 on v1

--- a/solution.py
+++ b/solution.py
@@ -23,7 +23,7 @@
     rhs, diag, back, fore, link, coup, base, w, xs, prod, pack, part, first, second,
     pick,
     near_u0, near_u1, near_u2, near_u3, near_d0, near_d1, near_d2, near_d3,
-    load_sem, up_s, up_r, dn_s, dn_r, f1_s, f1_r, f2_s, f2_r,
+    load_sem, up_s, up_r, dn_s, dn_r, f1_s, f1_r, f2_s, f2_r, go_sem,
 ):
     p, d = lax.axis_index("plane"), lax.axis_index("dom")
     x, y = d // 4, d % 4
@@ -38,9 +38,13 @@
         )
     ]
     load_rhs, load_diag, load_back, load_link, load_fore = loads
+    load_diag.start()
+
+    @pl.when(p > 0)
+    def _():
+        load_back.start()
+
     load_rhs.start()
-    load_diag.start()
-    load_back.start()
 
     barrier = pltpu.get_barrier_semaphore()
 
@@ -68,27 +72,24 @@
     beside = jnp.where((d > 0) & (d < 15), 3, 2)
     planes = jnp.where((p > 0) & (p < 7), 2, 1)
 
-    def moves(k, step, src, near, ss, rs):
+    def move(act, k, c, step, src, near, ss, rs):
         def one(n, shift):
             return pltpu.make_async_remote_copy(
-                src_ref=src.at[k],
-                dst_ref=near[k].at[pl.ds(2 - 2 * shift, 2)],
-                send_sem=ss.at[k, n],
-                recv_sem=rs.at[k, n],
+                src_ref=src.at[k, c],
+                dst_ref=near[k].at[2 - 2 * shift + c],
+                send_sem=ss.at[k, c, n],
+                recv_sem=rs.at[k, c, n],
                 device_id={"plane": p + step, "dom": d + shift},
                 device_id_type=MESH,
             )
 
-        return one(0, 1), one(1, -1), one(2, 0)
-
-    def move(act, k, step, src, near, ss, rs):
-        right, left, same = moves(k, step, src, near, ss, rs)
+        right, left, same = one(0, 1), one(1, -1), one(2, 0)
         if act == "recv":
             pl.when(d > 0)(right.wait_recv)
             pl.when(d < 15)(left.wait_recv)
             same.wait_recv()
         else:
-            do = (lambda c: c.start()) if act == "start" else (lambda c: c.wait_send())
+            do = (lambda m: m.start()) if act == "start" else (lambda m: m.wait_send())
             pl.when(d < 15)(lambda: do(right))
             pl.when(d > 0)(lambda: do(left))
             do(same)
@@ -99,25 +100,6 @@
     def spot(table, c, s):
         start = (d - 1) * 2
         return jnp.clip(start + table[0, c, s], 0, 31) - start
-
-    load_rhs.wait()
-    load_diag.wait()
-    for c in range(2):
-        whole = dot(rhs[c].astype(BF), diag[c])
-        for k in range(PIECES):
-            base[k, c] = whole[k * ROWS:(k + 1) * ROWS]
-
-    pl.semaphore_wait(barrier, beside * planes + 6)
-
-    @pl.when(p == 0)
-    def _():
-        for k in range(PIECES):
-            w[k] = base[k].astype(BF)
-            up("start", k)
-
-    load_back.wait()
-    load_link.start()
-    load_fore.start()
 
     def compose(src, dst):
         def body(i, _):
@@ -126,7 +108,30 @@
 
         lax.fori_loop(0, 4, body, 0)
 
-    pl.when(p > 0)(lambda: compose(back, coup))
+    load_diag.wait()
+
+    @pl.when(p > 0)
+    def _():
+        load_back.wait()
+        compose(back, coup)
+
+    load_rhs.wait()
+    for c in range(2):
+        whole = dot(rhs[c].astype(BF), diag[c])
+        for k in range(PIECES):
+            base[k, c] = whole[k * ROWS:(k + 1) * ROWS]
+
+    pl.semaphore_wait(barrier, beside * planes + 6)
+
+    @pl.when(p == 0)
+    def _():
+        for k in range(PIECES):
+            for c in range(2):
+                w[k, c] = base[k, c].astype(BF)
+                up("start", k, c)
+
+    load_link.start()
+    load_fore.start()
 
     def choose(i, _):
         one, two = jnp.int32(links), jnp.int32(links)
@@ -138,22 +143,25 @@
         pick[1, i] = two
         return 0
 
-    lax.fori_loop(0, 32, choose, 0)
-    for k in range(PIECES):
-        prod[k, links] = jnp.zeros((ROWS, 640), BF)
-
-    @pl.when(p >= 3)
-    def _():
+    def ready():
+        lax.fori_loop(0, 32, choose, 0)
+        for k in range(PIECES):
+            prod[k, links] = jnp.zeros((ROWS, 640), BF)
         load_fore.wait()
         pl.when(p < 7)(lambda: compose(fore, back))
 
-    def up_step(k):
-        up("recv", k)
+    pl.when(p >= 3)(ready)
+
+    def up_step(k, send=False):
+        for c in range(2):
+            up("recv", k, c)
         for c in range(2):
             total = base[k, c]
             for s in range(2):
                 total = total - dot(near_u[k][spot(back_near, c, s)], coup[c, s])
             w[k, c] = total.astype(BF)
+            if send:
+                up("start", k, c)
 
     def products(ks):
         def body(l, _):
@@ -163,7 +171,7 @@
                 prod[k, l] = got[i * ROWS:(i + 1) * ROWS]
             return 0
 
-        lax.fori_loop(0, links, body, 0)
+        lax.fori_loop(0, links, body, 0, unroll=4)
 
     def phase1(k):
         a = y if k % 2 == 0 else x
@@ -205,7 +213,7 @@
             pack[k, a, b, c] = both.astype(BF)
             return 0
 
-        lax.fori_loop(0, 32, body, 0)
+        lax.fori_loop(0, 32, body, 0, unroll=8)
         for copy in phase1(k)[1]:
             copy.start()
 
@@ -222,7 +230,7 @@
                 part[k, b, c] = total.astype(BF)
             return 0
 
-        lax.fori_loop(0, 4, body, 0)
+        lax.fori_loop(0, 4, body, 0, unroll=2)
         for copy in phase2(k)[1]:
             copy.start()
 
@@ -244,26 +252,32 @@
     def turn(k):
         for c in range(2):
             finish(k, c, base[k, c])
-        down("start", k)
+            down("start", k, c)
 
     def down_step(k):
-        down("recv", k)
+        for c in range(2):
+            down("recv", k, c)
         for c in range(2):
             total = base[k, c]
             for s in range(2):
                 total = total - dot(near_d[k][spot(fore_near, c, s)], back[c, s])
             finish(k, c, total)
-        pl.when(p > 0)(lambda: down("start", k))
+            pl.when(p > 0)(lambda: down("start", k, c))
 
     @pl.when(p == 7)
     def _():
         load_link.wait()
-        for k in range(PIECES):
+        for k in (0, 2):
             up_step(k)
-            products((k,))
+            up_step(k + 1)
+            products((k, k + 1))
             send_first(k)
-            if k >= 2:
-                send_second(k - 2)
+            send_first(k + 1)
+        pl.semaphore_signal(
+            go_sem, inc=1, device_id={"plane": p - 1, "dom": d}, device_id_type=MESH
+        )
+        send_second(0)
+        send_second(1)
         for k in range(PIECES):
             settle(k)
             turn(k)
@@ -275,28 +289,26 @@
         @pl.when(p > 0)
         def _():
             for k in range(PIECES):
-                up_step(k)
-                up("start", k)
-
+                up_step(k, True)
+
+        pl.when(p < 3)(ready)
         load_link.wait()
         products(tuple(range(PIECES)))
         for k in range(PIECES):
+            if k == 2:
+                pl.when(p == 6)(lambda: pl.semaphore_wait(go_sem, 1))
             send_first(k)
         for k in range(PIECES):
             send_second(k)
-
-        @pl.when(p < 3)
-        def _():
-            load_fore.wait()
-            compose(fore, back)
 
         for k in range(PIECES):
             settle(k)
             down_step(k)
 
     for k in range(PIECES):
-        pl.when(p < 7)(lambda: up("sent", k))
-        pl.when(p > 0)(lambda: down("sent", k))
+        for c in range(2):
+            pl.when(p < 7)(lambda: up("sent", k, c))
+            pl.when(p > 0)(lambda: down("sent", k, c))
         for copy in phase1(k)[1] + phase2(k)[1]:
             copy.wait_send()
 
@@ -305,12 +317,13 @@
     links = link.shape[1]
     piece = (PIECES, 2, ROWS, 640)
     near = pltpu.VMEM((6, ROWS, 640), BF)
+    each = pltpu.SemaphoreType.DMA((PIECES, 2, 3))
     sems = pltpu.SemaphoreType.DMA((PIECES, 3))
     anywhere = pl.BlockSpec(memory_space=pl.ANY)
     scalars = pl.BlockSpec(memory_space=pltpu.SMEM)
     return pl.pallas_call(
         kernel,
-        out_shape=jax.ShapeDtypeStruct(rhs.shape, BF),
+        out_shape=pltpu.VMEM(rhs.shape, BF),
         in_specs=[anywhere] * 5 + [scalars] * 5,
         out_specs=pl.BlockSpec(memory_space=pltpu.VMEM),
         scratch_shapes=[
@@ -332,7 +345,9 @@
         ]
         + [near] * (2 * PIECES)
         + [pltpu.SemaphoreType.DMA((5,))]
-        + [sems] * 8,
+        + [each] * 4
+        + [sems] * 4
+        + [pltpu.SemaphoreType.REGULAR],
         compiler_params=pltpu.CompilerParams(
             collective_id=0, has_side_effects=True, vmem_limit_bytes=58 * 1024 * 1024
         ),

time: 103 us -> 96.4 us (0.936)
  Pallas kernels: 101 us -> 95.6 us
    pallas_call x1, Pallas kernels: 101 us -> 95.6 us  [local(): pl.pallas_call(kernel, out_shape=pltpu.VMEM(rhs.shape, BF), in_specs=[any...]
where the time goes in v2:
time: 96.4 us; the launch traced here: 96.2 us
  Pallas kernels  95.6 us (99%)
    pallas_call x1, Pallas kernels, local(): pl.pallas_call(kernel, out_shape=pltpu.VMEM(rhs.shape, BF), in_specs=[any...  95.6 us

profile of v2, /device:TPU:2, one launch (start us, length us, event | category | flops | bytes accessed | tf_op | source)
XLA Modules:
  0.0 96.2 jit_solution(16716439489916964232)
XLA Ops:
  0.0 95.6 %shard_map.100 = bf16[1,2,64,640]{3,2,1,0:T(8,128)(2,1)S(1)} custom-call(f32[1,2,64,640]{3,2,1,0:T(8,128)} %rhs_h.1, bf16[1,2,640,640]{3,2,1,0:T(8,128)(2,1)} %diag_h.1, bf16[1,2,2,640,640]{4,3,2,1,0:T(8,128)(2,1)} %back_h.1, bf16[1,2,2,640,640]{4,3,2,1,0:T(8,128)(2,1)} %fore_h.1, bf16[1,12,640,640]{3,2,1,0:T(8,128)(2,1)} %link_h.1, s32[1,2,2]{2,1,0:T(2,128)} %back_near.1, ...), custom_call_target="tpu_custom_call" | custom-call | flops 16777216000 | bytes 20000000 | tf_op jit(solution)/shard_map/pallas_call | solution.py:324
  95.6 0.7 copy.12

commit v3 on v2

--- a/solution.py
+++ b/solution.py
@@ -273,11 +273,11 @@
             products((k, k + 1))
             send_first(k)
             send_first(k + 1)
+        send_second(0)
+        send_second(1)
         pl.semaphore_signal(
             go_sem, inc=1, device_id={"plane": p - 1, "dom": d}, device_id_type=MESH
         )
-        send_second(0)
-        send_second(1)
         for k in range(PIECES):
             settle(k)
             turn(k)
@@ -301,8 +301,13 @@
         for k in range(PIECES):
             send_second(k)
 
-        for k in range(PIECES):
-            settle(k)
+        @pl.when(p < 6)
+        def _():
+            for k in range(PIECES):
+                settle(k)
+
+        for k in range(PIECES):
+            pl.when(p == 6)(lambda: settle(k))
             down_step(k)
 
     for k in range(PIECES):

time: 96.4 us -> 93.6 us (0.971)
  Pallas kernels: 95.6 us -> 92.7 us
    pallas_call x1, Pallas kernels: 95.6 us -> 92.7 us  [local(): pl.pallas_call(kernel, out_shape=pltpu.VMEM(rhs.shape, BF), in_specs=[any...]
where the time goes in v3:
time: 93.6 us; the launch traced here: 93.4 us
  Pallas kernels  92.7 us (99%)
    pallas_call x1, Pallas kernels, local(): pl.pallas_call(kernel, out_shape=pltpu.VMEM(rhs.shape, BF), in_specs=[any...  92.7 us

profile of v3, /device:TPU:2, one launch (start us, length us, event | category | flops | bytes accessed | tf_op | source)
XLA Modules:
  0.0 93.4 jit_solution(9972297503694044770)
XLA Ops:
  0.0 92.7 %shard_map.100 = bf16[1,2,64,640]{3,2,1,0:T(8,128)(2,1)S(1)} custom-call(f32[1,2,64,640]{3,2,1,0:T(8,128)} %rhs_h.1, bf16[1,2,640,640]{3,2,1,0:T(8,128)(2,1)} %diag_h.1, bf16[1,2,2,640,640]{4,3,2,1,0:T(8,128)(2,1)} %back_h.1, bf16[1,2,2,640,640]{4,3,2,1,0:T(8,128)(2,1)} %fore_h.1, bf16[1,12,640,640]{3,2,1,0:T(8,128)(2,1)} %link_h.1, s32[1,2,2]{2,1,0:T(2,128)} %back_near.1, ...), custom_call_target="tpu_custom_call" | custom-call | flops 16777216000 | bytes 20000000 | tf_op jit(solution)/shard_map/pallas_call | solution.py:329
  92.7 0.7 copy.12

commit v4 on v3

--- a/solution.py
+++ b/solution.py
@@ -150,7 +150,7 @@
         load_fore.wait()
         pl.when(p < 7)(lambda: compose(fore, back))
 
-    pl.when(p >= 3)(ready)
+    pl.when((p == 3) | (p > 4))(ready)
 
     def up_step(k, send=False):
         for c in range(2):
@@ -171,7 +171,7 @@
                 prod[k, l] = got[i * ROWS:(i + 1) * ROWS]
             return 0
 
-        lax.fori_loop(0, links, body, 0, unroll=4)
+        lax.fori_loop(0, links, body, 0, unroll=12)
 
     def phase1(k):
         a = y if k % 2 == 0 else x
@@ -206,15 +206,12 @@
         return b, found
 
     def send_first(k):
-        def body(i, _):
+        for i in range(32):
             a, b, c = i // 8, (i // 2) % 4, i % 2
             cell = (b * 4 + a) * 2 + c if k % 2 == 0 else i
-            both = prod[k, pick[0, cell]].astype(F32) + prod[k, pick[1, cell]].astype(F32)
-            pack[k, a, b, c] = both.astype(BF)
-            return 0
-
-        lax.fori_loop(0, 32, body, 0, unroll=8)
-        for copy in phase1(k)[1]:
+            pack[k, a, b, c] = prod[k, pick[0, cell]] + prod[k, pick[1, cell]]
+        one, two, three = phase1(k)[1]
+        for copy in (one, three, two):
             copy.start()
 
     def send_second(k):
@@ -222,16 +219,14 @@
         for copy in copies:
             copy.wait_recv()
 
-        def body(b, _):
+        for b in range(4):
             for c in range(2):
                 total = pack[k, a, b, c].astype(F32)
                 for j in range(3):
                     total = total + first[k, j, b, c].astype(F32)
                 part[k, b, c] = total.astype(BF)
-            return 0
-
-        lax.fori_loop(0, 4, body, 0, unroll=2)
-        for copy in phase2(k)[1]:
+        one, two, three = phase2(k)[1]
+        for copy in (one, three, two):
             copy.start()
 
     def settle(k):
@@ -254,7 +249,7 @@
             finish(k, c, base[k, c])
             down("start", k, c)
 
-    def down_step(k):
+    def down_step(k, send):
         for c in range(2):
             down("recv", k, c)
         for c in range(2):
@@ -262,7 +257,8 @@
             for s in range(2):
                 total = total - dot(near_d[k][spot(fore_near, c, s)], back[c, s])
             finish(k, c, total)
-            pl.when(p > 0)(lambda: down("start", k, c))
+            if send:
+                down("start", k, c)
 
     @pl.when(p == 7)
     def _():
@@ -291,7 +287,7 @@
             for k in range(PIECES):
                 up_step(k, True)
 
-        pl.when(p < 3)(ready)
+        pl.when((p < 3) | (p == 4))(ready)
         load_link.wait()
         products(tuple(range(PIECES)))
         for k in range(PIECES):
@@ -306,9 +302,21 @@
             for k in range(PIECES):
                 settle(k)
 
-        for k in range(PIECES):
-            pl.when(p == 6)(lambda: settle(k))
-            down_step(k)
+        @pl.when(p == 6)
+        def _():
+            for k in range(PIECES):
+                settle(k)
+                down_step(k, True)
+
+        @pl.when((p > 0) & (p < 6))
+        def _():
+            for k in range(PIECES):
+                down_step(k, True)
+
+        @pl.when(p == 0)
+        def _():
+            for k in range(PIECES):
+                down_step(k, False)
 
     for k in range(PIECES):
         for c in range(2):

time: 93.6 us -> 92.4 us (0.987)
  Pallas kernels: 92.7 us -> 91.5 us
    pallas_call x1, Pallas kernels: 92.7 us -> 91.5 us  [local(): pl.pallas_call(kernel, out_shape=pltpu.VMEM(rhs.shape, BF), in_specs=[any...]
where the time goes in v4:
time: 92.4 us; the launch traced here: 92.2 us
  Pallas kernels  91.5 us (99%)
    pallas_call x1, Pallas kernels, local(): pl.pallas_call(kernel, out_shape=pltpu.VMEM(rhs.shape, BF), in_specs=[any...  91.5 us

profile of v4, /device:TPU:2, one launch (start us, length us, event | category | flops | bytes accessed | tf_op | source)
XLA Modules:
  0.0 92.2 jit_solution(9289841551843058705)
XLA Ops:
  0.0 91.5 %shard_map.100 = bf16[1,2,64,640]{3,2,1,0:T(8,128)(2,1)S(1)} custom-call(f32[1,2,64,640]{3,2,1,0:T(8,128)} %rhs_h.1, bf16[1,2,640,640]{3,2,1,0:T(8,128)(2,1)} %diag_h.1, bf16[1,2,2,640,640]{4,3,2,1,0:T(8,128)(2,1)} %back_h.1, bf16[1,2,2,640,640]{4,3,2,1,0:T(8,128)(2,1)} %fore_h.1, bf16[1,12,640,640]{3,2,1,0:T(8,128)(2,1)} %link_h.1, s32[1,2,2]{2,1,0:T(2,128)} %back_near.1, ...), custom_call_target="tpu_custom_call" | custom-call | flops 16777216000 | bytes 20000000 | tf_op jit(solution)/shard_map/pallas_call | solution.py:337
  91.5 0.7 copy.12

commit v5 on v4

--- a/solution.py
+++ b/solution.py
@@ -90,9 +90,9 @@
             same.wait_recv()
         else:
             do = (lambda m: m.start()) if act == "start" else (lambda m: m.wait_send())
+            do(same)
             pl.when(d < 15)(lambda: do(right))
             pl.when(d > 0)(lambda: do(left))
-            do(same)
 
     up = functools.partial(move, step=1, src=w, near=near_u, ss=up_s, rs=up_r)
     down = functools.partial(move, step=-1, src=xs, near=near_d, ss=dn_s, rs=dn_r)

time: 92.4 us -> 92.4 us (level)
  no operation moved by 1% of the time
where the time goes in v5:
time: 92.4 us; the launch traced here: 92.2 us
  Pallas kernels  91.5 us (99%)
    pallas_call x1, Pallas kernels, local(): pl.pallas_call(kernel, out_shape=pltpu.VMEM(rhs.shape, BF), in_specs=[any...  91.5 us

profile of v5, /device:TPU:2, one launch (start us, length us, event | category | flops | bytes accessed | tf_op | source)
XLA Modules:
  0.0 92.2 jit_solution(14136320418365576724)
XLA Ops:
  0.0 91.5 %shard_map.100 = bf16[1,2,64,640]{3,2,1,0:T(8,128)(2,1)S(1)} custom-call(f32[1,2,64,640]{3,2,1,0:T(8,128)} %rhs_h.1, bf16[1,2,640,640]{3,2,1,0:T(8,128)(2,1)} %diag_h.1, bf16[1,2,2,640,640]{4,3,2,1,0:T(8,128)(2,1)} %back_h.1, bf16[1,2,2,640,640]{4,3,2,1,0:T(8,128)(2,1)} %fore_h.1, bf16[1,12,640,640]{3,2,1,0:T(8,128)(2,1)} %link_h.1, s32[1,2,2]{2,1,0:T(2,128)} %back_near.1, ...), custom_call_target="tpu_custom_call" | custom-call | flops 16777216000 | bytes 20000000 | tf_op jit(solution)/shard_map/pallas_call | solution.py:337
  91.6 0.7 copy.12
